TPU v7x, 32 devices: a whole 2x2x4 slice. The times are simulated.
32 devices in a mesh: gx: 8 (over y, x, core), gy: 4 (over z).
Axes of the slice: x: 2, y: 2, z: 4, core: 2. Of those that a mesh axis runs over, the one named last changes fastest.
Arguments:
- particles: float32 [8, 4, 128, 8, 128], P('gx', 'gy'), may hold values from -4 to 4, as said below
- send_list: int32 [8, 4, 4, 64], P('gx', 'gy'), may hold values from 0 to 127, as said below
- move_count: int32 [8, 4, 2, 4], P('gx', 'gy'), may hold values from 0 to 16, as said below
- tile_pairs: int32 [8, 4, 512, 2], P('gx', 'gy'), may hold values from 0 to 383, as said below
- tile_count: int32 [8, 4], P('gx', 'gy'), may hold values from 128 to 512, as said below
- drag_tiles: int32 [8, 4, 384, 4], P('gx', 'gy'), may hold values from 0 to 99, as said below
- cell_slot: int32 [8, 4, 384, 128], P('gx', 'gy'), may hold values from 0 to 511
- fluid_velocity: float32 [3, 64, 32, 128], P(None, 'gx', 'gy'), may hold values from -6 to 6
- pressure_init: float32 [64, 32, 128], P('gx', 'gy'), may hold values from -6 to 6
- source: float32 [64, 32, 128], P('gx', 'gy'), may hold values from -6 to 6
- solid_old: float32 [64, 32, 128], P('gx', 'gy'), may hold values from 0 to 0.5
- screening: float32 [64, 32, 128], P('gx', 'gy'), may hold values from 0.5 to 2
Outputs:
- pressure: float32 [64, 32, 128], P('gx', 'gy')
- drag_sum: float32 [3, 64, 32, 128], P(None, 'gx', 'gy')
- block_force: float32 [8, 4, 384, 3, 128], P('gx', 'gy')
Inputs may be any that keep to these rules, and one draw needn't show every extreme that they name: `particles`: positions lie in 0 to 3, radii in 0.3 to 0.7, drag coefficients in 0.5 to 4. `send_list`: row d of a device sends toward the neighbour of higher gx (d 0), lower gx (1), higher gy (2), lower gy (3). Its first move_count[0, d] entries are blocks that move there, all different over the four rows; the others are copies, and every slot is sent. `move_count`: entry [0, d] counts blocks leaving in direction d of send_list; entry [1, d] equals entry [0, d] of the neighbour that feeds received group d (lower gx, higher gx, lower gy, higher gy). Counts toward or from outside the grid are 0; 16 is reached in every draw. `tile_pairs`: the first block of every tile slot is owned by the device after migration; the second is an own block or a slot received from a neighbour inside the grid. `tile_count`: devices at the lowest and highest gy use all 512 tiles. `drag_tiles`: the 4 columns of a block are different.
All inputs are finite; a program needn't handle non-finite values.
Results may differ from a plain program's by a relative error of at most 0.0003.
Values sent between devices are 32-bit elements; how exact they have to be, the bound alone decides.
A program may use at most 64 MiB of HBM per device.

v0:
```python
import jax
import jax.numpy as jnp
from jax import lax
from jax.sharding import PartitionSpec as P

ITERS = 4


topmost_value = lax.Precision.HIGHEST
stiffness = 0.5
density_ratio = 2.0
tile_group = 32
block_groups = 6


def extended_2(block, sides, width):
    for axis, dim in sides:
        count = lax.axis_size(axis)
        forward = [(i, i + 1) for i in range(count - 1)]
        backward = [(target, source) for source, target in forward]
        low = lax.ppermute(
            lax.slice_in_dim(block, block.shape[dim] - width, None, axis=dim), axis, forward
        )
        high = lax.ppermute(lax.slice_in_dim(block, 0, width, axis=dim), axis, backward)
        block = jnp.concatenate([low, block, high], axis=dim)
    return block


def ownership(send_rows, leave_count, arrive_count, block_count):
    slot_count = send_rows.shape[1]
    slot_iota = jnp.arange(slot_count, dtype=jnp.int32)
    leaving = (send_rows[:, :, None] == jnp.arange(block_count, dtype=jnp.int32)[None, None, :]) & (
        slot_iota[None, :, None] < leave_count[:, None, None]
    )
    stayed = jnp.logical_not(jnp.any(leaving, axis=(0, 1)))
    arrived = slot_iota[None, :] < arrive_count[:, None]
    return jnp.concatenate([stayed, arrived.reshape(-1)]).astype(jnp.float32)


def contact_forces(block_pool, tile_rows, tile_total):
    slot_total = tile_rows.shape[0]
    grouped = tile_rows.reshape(slot_total // tile_group, tile_group, 2)
    marks = (
        (jnp.arange(slot_total, dtype=jnp.int32) < tile_total)
        .astype(jnp.float32)
        .reshape(-1, tile_group)
    )

    def tile_step(force_total, step_item):
        pair_group, mark_group = step_item
        first_side = block_pool[pair_group[:, 0], 0:4, :]
        second_side = block_pool[pair_group[:, 1], 0:4, :]
        distance = (first_side[:, 0, :, None] - second_side[:, 0, None, :]) ** 2
        distance = distance + (first_side[:, 1, :, None] - second_side[:, 1, None, :]) ** 2
        distance = distance + (first_side[:, 2, :, None] - second_side[:, 2, None, :]) ** 2
        reach = first_side[:, 3, :, None] + second_side[:, 3, None, :]
        weight = jnp.maximum(1.0 - distance / (reach * reach), 0.0) * mark_group[:, None, None]
        pulled = jnp.einsum("tab,tcb->tca", weight, second_side[:, 0:3, :], precision=topmost_value)
        pushed = first_side[:, 0:3, :] * jnp.sum(weight, axis=2)[:, None, :]
        return (force_total.at[pair_group[:, 0]].add(stiffness * (pushed - pulled)), None)

    start_force = jnp.zeros((block_pool.shape[0], 3, block_pool.shape[2]), jnp.float32)
    force_total, unused = lax.scan(tile_step, start_force, (grouped, marks))
    return force_total


def couple(block_pool, owned_mask, tile_ids, slot_ids, columns):
    depth_count = columns.shape[2]
    column_count = columns.shape[0]
    tile_width = tile_ids.shape[1]
    per_group = block_pool.shape[0] // block_groups

    def group_advance(deposit, step_item):
        block_state, owned_rows, group_tiles, group_slots = step_item
        depth_ids = group_slots % depth_count
        slot_tile = group_slots // depth_count
        depth_pick = (
            depth_ids[:, :, None] == jnp.arange(depth_count, dtype=jnp.int32)[None, None, :]
        ).astype(jnp.float32)
        slot_selection = (
            slot_tile[:, :, None] == jnp.arange(tile_width, dtype=jnp.int32)[None, None, :]
        ).astype(jnp.float32)
        local_flow = columns[group_tiles]
        depth_position = jnp.einsum(
            "gkcz,gpz->gkcp", local_flow, depth_pick, precision=topmost_value
        )
        fluid_sampled_locally = jnp.einsum(
            "hxdq,hqx->hdq", depth_position, slot_selection, precision=topmost_value
        )
        drag_force = (
            block_state[:, 7:8, :]
            * (fluid_sampled_locally - block_state[:, 4:7, :])
            * owned_rows[:, None, None]
        )
        volume = block_state[:, 3:4, :] ** 3 * owned_rows[:, None, None]
        loading_contributions = jnp.concatenate([drag_force, volume], axis=1)
        slot_breakdown = jnp.einsum(
            "bfm,bmd->bdfm", loading_contributions, slot_selection, precision=topmost_value
        )
        spread = jnp.einsum("gkcp,gpz->gkcz", slot_breakdown, depth_pick, precision=topmost_value)
        column_pick = (
            group_tiles[:, :, None] == jnp.arange(column_count, dtype=jnp.int32)[None, None, :]
        ).astype(jnp.float32)
        deposit = deposit + jnp.einsum(
            "gkn,gkcz->ncz", column_pick, spread, precision=topmost_value
        )
        return (deposit, drag_force)

    step_items = (
        block_pool.reshape(block_groups, per_group, block_pool.shape[1], block_pool.shape[2]),
        owned_mask.reshape(block_groups, per_group),
        tile_ids.reshape(block_groups, per_group, tile_width),
        slot_ids.reshape(block_groups, per_group, slot_ids.shape[1]),
    )
    start_deposit = jnp.zeros((column_count, 4, depth_count), jnp.float32)
    deposit, drag_force = lax.scan(group_advance, start_deposit, step_items)
    return (drag_force.reshape(block_pool.shape[0], 3, block_pool.shape[2]), deposit)


def relax(padded, relax_gain, offset):
    full = jnp.pad(padded, ((0, 0), (0, 0), (1, 1)))
    neighbours = full[2:, 1:-1, 1:-1] + full[:-2, 1:-1, 1:-1]
    neighbours = neighbours + full[1:-1, 2:, 1:-1] + full[1:-1, :-2, 1:-1]
    neighbours = neighbours + full[1:-1, 1:-1, 2:] + full[1:-1, 1:-1, :-2]
    return relax_gain * neighbours + offset


def fold_rims(spread):
    core = spread[:, 2:-2, 2:-2]
    core = core.at[:, 0, :].add(spread[:, 0, 2:-2])
    core = core.at[:, -1, :].add(spread[:, -1, 2:-2])
    core = core.at[:, :, 0].add(spread[:, 2:-2, 0])
    core = core.at[:, :, -1].add(spread[:, 2:-2, -1])
    core = core.at[:, 0, 0].add(spread[:, 0, 0])
    core = core.at[:, 0, -1].add(spread[:, 0, -1])
    core = core.at[:, -1, 0].add(spread[:, -1, 0])
    core = core.at[:, -1, -1].add(spread[:, -1, -1])
    return core


def body(
    particles,
    send_list,
    move_count,
    tile_pairs,
    tile_count,
    drag_tiles,
    cell_slot,
    fluid_velocity,
    pressure_init,
    source,
    solid_old,
    screening,
):
    own_blocks = particles[0, 0]
    send_rows = send_list[0, 0]
    outgoing = own_blocks[send_rows]
    axial_out = jnp.stack([outgoing[1], outgoing[0]])
    radial_out = jnp.stack([outgoing[3], outgoing[2]])
    axial_in = extended_2(axial_out, (("gx", 0),), 1)
    radial_in = extended_2(radial_out, (("gy", 0),), 1)
    block_pool = jnp.concatenate(
        [own_blocks, axial_in[0], axial_in[3], radial_in[0], radial_in[3]], axis=0
    )
    owned_mask = ownership(send_rows, move_count[0, 0, 0], move_count[0, 0, 1], own_blocks.shape[0])
    contact = contact_forces(block_pool, tile_pairs[0, 0], tile_count[0, 0])
    cells_x = pressure_init.shape[0]
    cells_y = pressure_init.shape[1]
    depth_count = pressure_init.shape[2]
    column_count = (cells_x + 2) * (cells_y + 2)
    flow_rim = extended_2(fluid_velocity, (("gx", 1), ("gy", 2)), 1)
    columns = flow_rim.reshape(3, column_count, depth_count).transpose(1, 0, 2)
    drag_force, deposit = couple(block_pool, owned_mask, drag_tiles[0, 0], cell_slot[0, 0], columns)
    block_force = contact + drag_force
    extended = deposit.transpose(1, 0, 2).reshape(4, cells_x + 2, cells_y + 2, depth_count)
    gathered = extended_2(extended, (("gx", 1), ("gy", 2)), 1)
    loads = fold_rims(gathered)
    drag_sum = loads[0:3]
    relax_gain = 1.0 / (6.0 + screening)
    offset = relax_gain * (source + density_ratio * (loads[3] - solid_old))
    pressure = pressure_init
    for sweep_turn in range(ITERS):
        padded = extended_2(pressure, (("gx", 0), ("gy", 1)), 1)
        pressure = relax(padded, relax_gain, offset)
    return (pressure, drag_sum, block_force[None, None])


def solution(mesh):
    in_specs = (
        P("gx", "gy", None, None, None),
        P("gx", "gy", None, None),
        P("gx", "gy", None, None),
        P("gx", "gy", None, None),
        P("gx", "gy"),
        P("gx", "gy", None, None),
        P("gx", "gy", None, None),
        P(None, "gx", "gy", None),
        P("gx", "gy", None),
        P("gx", "gy", None),
        P("gx", "gy", None),
        P("gx", "gy", None),
    )
    out_specs = (P("gx", "gy", None), P(None, "gx", "gy", None), P("gx", "gy", None, None, None))
    return jax.shard_map(body, mesh=mesh, in_specs=in_specs, out_specs=out_specs, check_vma=False)
```

profile of v0, /device:TPU:12, one launch (start us, length us, event | category | flops | bytes accessed | tf_op | source)
XLA Modules:
  0.0 393.2 jit_solution(14206459176418863082)
XLA Ops:
  6.1 4.5 %collective-permute-start.5 = (f32[1,64,8,128]{3,2,1,0:T(8,128)}, f32[1,64,8,128]{3,2,1,0:T(8,128)S(1)}, u32[]{:S(2)}, u32[]{:S(2)}) collective-permute-start(f32[1,64,8,128]{3,2,1,0:T(8,128)} %get-tuple-element.392), channel_id=1, source_target_pairs={{4,0},{8,4},{12,8},{16,12},{20,16},{24,20},{28,24},{5,1},{9,5},{13... | collective-permute-start | bytes 786440 | tf_op jit(solution)/shard_map/ppermute | solution.py:24
  10.6 3.5 collective-permute-start.6
  16.1 2.6 collective-permute-start.1
  21.9 3.3 collective-permute-start
  26.5 4.5 %collective-permute-start.9 = (f32[3,1,8,128]{3,2,1,0:T(8,128)S(1)}, f32[3,1,8,128]{3,2,1,0:T(8,128)S(1)}, u32[]{:S(2)}, u32[]{:S(2)}) collective-permute-start(f32[3,1,8,128]{3,2,1,0:T(8,128)S(1)} %get-tuple-element.400), channel_id=1, source_target_pairs={{4,0},{8,4},{12,8},{16,12},{20,16},{24,20},{28,24},{5,1},{9,5},{13... | collective-permute-start | bytes 36872 | tf_op jit(solution)/shard_map/ppermute | solution.py:24
  32.4 3.5 collective-permute-start.10
  44.1 3.6 collective-permute-start.3
  47.9 73.5 %while.34 = (s32[]{:T(128)}, f32[100,4,128]{2,0,1:T(8,128)S(1)}, f32[6,64,3,128]{3,1,0,2:T(8,128)}, s32[6,64,4]{1,0,2:T(8,128)S(1)}, s32[6,64,128]{2,1,0:T(8,128...) while((s32[]{:T(128)}, f32[100,4,128]{2,0,1:T(8,128)S(1)}, ...), condition=%wide.region_2.3_spmd.clone, body=%wide.region_1.2_spmd.clone.sunk | while | flops 512539392 | bytes 5653123 | solution.py:116
  50.7 4.1 %fusion.106 = f32[64,128,3]{1,2,0:T(4,128)S(1)} fusion(f32[64,4,3,128]{3,2,1,0:T(4,128)S(1)} %bitcast.196, s32[64,128]{1,0:T(8,128)S(1)} %add_select_fusion.6, f32[64,128,4]{1,2,0:T(4,128)S(1)} %fusion.105), kind=kOutput, calls=%fused_computation.38.clone.1 | convolution fusion | flops 152215552 | bytes 655360 | tf_op jit(solution)/shard_map/while/body/eval_jaxpr/gkcz,gpz->gkcp/dot_general | solution.py:84
  56.6 3.0 fusion.107
  63.0 4.1 %fusion.106 = f32[64,128,3]{1,2,0:T(4,128)S(1)} fusion(f32[64,4,3,128]{3,2,1,0:T(4,128)S(1)} %bitcast.196, s32[64,128]{1,0:T(8,128)S(1)} %add_select_fusion.6, f32[64,128,4]{1,2,0:T(4,128)S(1)} %fusion.105), kind=kOutput, calls=%fused_computation.38.clone.1 | convolution fusion | flops 152215552 | bytes 655360 | tf_op jit(solution)/shard_map/while/body/eval_jaxpr/gkcz,gpz->gkcp/dot_general | solution.py:84
  68.8 3.0 fusion.107
  75.2 4.1 %fusion.106 = f32[64,128,3]{1,2,0:T(4,128)S(1)} fusion(f32[64,4,3,128]{3,2,1,0:T(4,128)S(1)} %bitcast.196, s32[64,128]{1,0:T(8,128)S(1)} %add_select_fusion.6, f32[64,128,4]{1,2,0:T(4,128)S(1)} %fusion.105), kind=kOutput, calls=%fused_computation.38.clone.1 | convolution fusion | flops 152215552 | bytes 655360 | tf_op jit(solution)/shard_map/while/body/eval_jaxpr/gkcz,gpz->gkcp/dot_general | solution.py:84
  81.1 3.0 fusion.107
  87.5 4.1 %fusion.106 = f32[64,128,3]{1,2,0:T(4,128)S(1)} fusion(f32[64,4,3,128]{3,2,1,0:T(4,128)S(1)} %bitcast.196, s32[64,128]{1,0:T(8,128)S(1)} %add_select_fusion.6, f32[64,128,4]{1,2,0:T(4,128)S(1)} %fusion.105), kind=kOutput, calls=%fused_computation.38.clone.1 | convolution fusion | flops 152215552 | bytes 655360 | tf_op jit(solution)/shard_map/while/body/eval_jaxpr/gkcz,gpz->gkcp/dot_general | solution.py:84
  93.3 3.0 fusion.107
  99.7 4.1 %fusion.106 = f32[64,128,3]{1,2,0:T(4,128)S(1)} fusion(f32[64,4,3,128]{3,2,1,0:T(4,128)S(1)} %bitcast.196, s32[64,128]{1,0:T(8,128)S(1)} %add_select_fusion.6, f32[64,128,4]{1,2,0:T(4,128)S(1)} %fusion.105), kind=kOutput, calls=%fused_computation.38.clone.1 | convolution fusion | flops 152215552 | bytes 655360 | tf_op jit(solution)/shard_map/while/body/eval_jaxpr/gkcz,gpz->gkcp/dot_general | solution.py:84
  105.5 3.0 fusion.107
  111.9 4.1 %fusion.106 = f32[64,128,3]{1,2,0:T(4,128)S(1)} fusion(f32[64,4,3,128]{3,2,1,0:T(4,128)S(1)} %bitcast.196, s32[64,128]{1,0:T(8,128)S(1)} %add_select_fusion.6, f32[64,128,4]{1,2,0:T(4,128)S(1)} %fusion.105), kind=kOutput, calls=%fused_computation.38.clone.1 | convolution fusion | flops 152215552 | bytes 655360 | tf_op jit(solution)/shard_map/while/body/eval_jaxpr/gkcz,gpz->gkcp/dot_general | solution.py:84
  117.8 3.0 fusion.107
  123.4 4.5 %collective-permute-start.13 = (f32[4,1,10,128]{3,0,2,1:T(4,128)S(1)}, f32[4,1,10,128]{3,0,2,1:T(4,128)S(1)}, u32[]{:S(2)}, u32[]{:S(2)}) collective-permute-start(f32[4,1,10,128]{3,0,2,1:T(4,128)S(1)} %get-tuple-element.396), channel_id=1, source_target_pairs={{4,0},{8,4},{12,8},{16,12},{20,16},{24,20},{28,24},{5,1},{9,5},{13... | collective-permute-start | bytes 61448 | tf_op jit(solution)/shard_map/ppermute | solution.py:24
  129.4 2.5 collective-permute-start.14
  131.9 3.4 collective-permute-start.15
  139.8 3.1 collective-permute-start.16
  144.8 3.9 collective-permute-done.17
  148.7 3.4 collective-permute-start.18
  152.1 2.5 collective-permute-start.19
  154.6 3.0 collective-permute-done.19
  162.9 2.8 collective-permute-done.21
  167.6 3.9 collective-permute-start.23
  177.8 206.0 %while.33 = (s32[]{:T(128)}, f32[384,3,128]{2,1,0:T(4,128)S(1)}, s32[16,32,2]{1,0,2:T(8,128)S(1)}, f32[384,8,128]{2,0,1:T(8,128)S(1)}, f32[16,32]{1,0:T(8,128)S(1)}, /*index=5*/s32[]{:T(128)}) while((s32[]{:T(128)}, f32[384,3,128]{2,1,0:T(4,128)S(1)}, s32[16,32,2]{1,0,2:T(8,128)S(1)}, f32[384,8,128]{2,0,1:T(8,128)S(1)}, ...), condition=%wide.region_7.8_spmd, body=%wide.region_4.0_spmd.sunk | while | flops 34124096 | bytes 1313101 | solution.py:63
  179.2 3.3 fusion.96
  182.5 6.5 %fusion.97 = f32[32,3,128]{2,1,0:T(4,128)S(1)} fusion(f32[32]{0:T(128)S(1)} %dynamic-slice_bitcast_fusion.2, f32[32,128]{1,0:T(8,128)S(1)} %get-tuple-element.516, f32[32,128]{1,0:T(8,128)S(1)} %get-tuple-element.517, f32[32,128]{1,0:T(8,128)S(1)} %get-tuple-element.518, f32[32,128]{1,0:T(8,128)S(1)} %get-tuple-element.519, ...), kind=kOutput, calls=%fused_computation.7.clone.1 | convolution fusion | flops 26251264 | bytes 295040 | tf_op jit(solution)/shard_map/while/body/eval_jaxpr/tab,tcb->tca/dot_general | solution.py:58
  192.1 3.3 fusion.96
  195.4 6.5 %fusion.97 = f32[32,3,128]{2,1,0:T(4,128)S(1)} fusion(f32[32]{0:T(128)S(1)} %dynamic-slice_bitcast_fusion.2, f32[32,128]{1,0:T(8,128)S(1)} %get-tuple-element.516, f32[32,128]{1,0:T(8,128)S(1)} %get-tuple-element.517, f32[32,128]{1,0:T(8,128)S(1)} %get-tuple-element.518, f32[32,128]{1,0:T(8,128)S(1)} %get-tuple-element.519, ...), kind=kOutput, calls=%fused_computation.7.clone.1 | convolution fusion | flops 26251264 | bytes 295040 | tf_op jit(solution)/shard_map/while/body/eval_jaxpr/tab,tcb->tca/dot_general | solution.py:58
  205.0 3.3 fusion.96
  208.3 6.5 %fusion.97 = f32[32,3,128]{2,1,0:T(4,128)S(1)} fusion(f32[32]{0:T(128)S(1)} %dynamic-slice_bitcast_fusion.2, f32[32,128]{1,0:T(8,128)S(1)} %get-tuple-element.516, f32[32,128]{1,0:T(8,128)S(1)} %get-tuple-element.517, f32[32,128]{1,0:T(8,128)S(1)} %get-tuple-element.518, f32[32,128]{1,0:T(8,128)S(1)} %get-tuple-element.519, ...), kind=kOutput, calls=%fused_computation.7.clone.1 | convolution fusion | flops 26251264 | bytes 295040 | tf_op jit(solution)/shard_map/while/body/eval_jaxpr/tab,tcb->tca/dot_general | solution.py:58
  217.9 3.3 fusion.96
  221.2 6.5 %fusion.97 = f32[32,3,128]{2,1,0:T(4,128)S(1)} fusion(f32[32]{0:T(128)S(1)} %dynamic-slice_bitcast_fusion.2, f32[32,128]{1,0:T(8,128)S(1)} %get-tuple-element.516, f32[32,128]{1,0:T(8,128)S(1)} %get-tuple-element.517, f32[32,128]{1,0:T(8,128)S(1)} %get-tuple-element.518, f32[32,128]{1,0:T(8,128)S(1)} %get-tuple-element.519, ...), kind=kOutput, calls=%fused_computation.7.clone.1 | convolution fusion | flops 26251264 | bytes 295040 | tf_op jit(solution)/shard_map/while/body/eval_jaxpr/tab,tcb->tca/dot_general | solution.py:58
  230.8 3.3 fusion.96
  234.1 6.5 %fusion.97 = f32[32,3,128]{2,1,0:T(4,128)S(1)} fusion(f32[32]{0:T(128)S(1)} %dynamic-slice_bitcast_fusion.2, f32[32,128]{1,0:T(8,128)S(1)} %get-tuple-element.516, f32[32,128]{1,0:T(8,128)S(1)} %get-tuple-element.517, f32[32,128]{1,0:T(8,128)S(1)} %get-tuple-element.518, f32[32,128]{1,0:T(8,128)S(1)} %get-tuple-element.519, ...), kind=kOutput, calls=%fused_computation.7.clone.1 | convolution fusion | flops 26251264 | bytes 295040 | tf_op jit(solution)/shard_map/while/body/eval_jaxpr/tab,tcb->tca/dot_general | solution.py:58
  243.6 3.3 fusion.96
  246.9 6.5 %fusion.97 = f32[32,3,128]{2,1,0:T(4,128)S(1)} fusion(f32[32]{0:T(128)S(1)} %dynamic-slice_bitcast_fusion.2, f32[32,128]{1,0:T(8,128)S(1)} %get-tuple-element.516, f32[32,128]{1,0:T(8,128)S(1)} %get-tuple-element.517, f32[32,128]{1,0:T(8,128)S(1)} %get-tuple-element.518, f32[32,128]{1,0:T(8,128)S(1)} %get-tuple-element.519, ...), kind=kOutput, calls=%fused_computation.7.clone.1 | convolution fusion | flops 26251264 | bytes 295040 | tf_op jit(solution)/shard_map/while/body/eval_jaxpr/tab,tcb->tca/dot_general | solution.py:58
  256.5 3.3 fusion.96
  259.8 6.5 %fusion.97 = f32[32,3,128]{2,1,0:T(4,128)S(1)} fusion(f32[32]{0:T(128)S(1)} %dynamic-slice_bitcast_fusion.2, f32[32,128]{1,0:T(8,128)S(1)} %get-tuple-element.516, f32[32,128]{1,0:T(8,128)S(1)} %get-tuple-element.517, f32[32,128]{1,0:T(8,128)S(1)} %get-tuple-element.518, f32[32,128]{1,0:T(8,128)S(1)} %get-tuple-element.519, ...), kind=kOutput, calls=%fused_computation.7.clone.1 | convolution fusion | flops 26251264 | bytes 295040 | tf_op jit(solution)/shard_map/while/body/eval_jaxpr/tab,tcb->tca/dot_general | solution.py:58
  269.4 3.3 fusion.96
  272.7 6.5 %fusion.97 = f32[32,3,128]{2,1,0:T(4,128)S(1)} fusion(f32[32]{0:T(128)S(1)} %dynamic-slice_bitcast_fusion.2, f32[32,128]{1,0:T(8,128)S(1)} %get-tuple-element.516, f32[32,128]{1,0:T(8,128)S(1)} %get-tuple-element.517, f32[32,128]{1,0:T(8,128)S(1)} %get-tuple-element.518, f32[32,128]{1,0:T(8,128)S(1)} %get-tuple-element.519, ...), kind=kOutput, calls=%fused_computation.7.clone.1 | convolution fusion | flops 26251264 | bytes 295040 | tf_op jit(solution)/shard_map/while/body/eval_jaxpr/tab,tcb->tca/dot_general | solution.py:58
  282.3 3.3 fusion.96
  285.6 6.5 %fusion.97 = f32[32,3,128]{2,1,0:T(4,128)S(1)} fusion(f32[32]{0:T(128)S(1)} %dynamic-slice_bitcast_fusion.2, f32[32,128]{1,0:T(8,128)S(1)} %get-tuple-element.516, f32[32,128]{1,0:T(8,128)S(1)} %get-tuple-element.517, f32[32,128]{1,0:T(8,128)S(1)} %get-tuple-element.518, f32[32,128]{1,0:T(8,128)S(1)} %get-tuple-element.519, ...), kind=kOutput, calls=%fused_computation.7.clone.1 | convolution fusion | flops 26251264 | bytes 295040 | tf_op jit(solution)/shard_map/while/body/eval_jaxpr/tab,tcb->tca/dot_general | solution.py:58
  295.1 3.3 fusion.96
  298.4 6.5 %fusion.97 = f32[32,3,128]{2,1,0:T(4,128)S(1)} fusion(f32[32]{0:T(128)S(1)} %dynamic-slice_bitcast_fusion.2, f32[32,128]{1,0:T(8,128)S(1)} %get-tuple-element.516, f32[32,128]{1,0:T(8,128)S(1)} %get-tuple-element.517, f32[32,128]{1,0:T(8,128)S(1)} %get-tuple-element.518, f32[32,128]{1,0:T(8,128)S(1)} %get-tuple-element.519, ...), kind=kOutput, calls=%fused_computation.7.clone.1 | convolution fusion | flops 26251264 | bytes 295040 | tf_op jit(solution)/shard_map/while/body/eval_jaxpr/tab,tcb->tca/dot_general | solution.py:58
  308.0 3.3 fusion.96
  311.3 6.5 %fusion.97 = f32[32,3,128]{2,1,0:T(4,128)S(1)} fusion(f32[32]{0:T(128)S(1)} %dynamic-slice_bitcast_fusion.2, f32[32,128]{1,0:T(8,128)S(1)} %get-tuple-element.516, f32[32,128]{1,0:T(8,128)S(1)} %get-tuple-element.517, f32[32,128]{1,0:T(8,128)S(1)} %get-tuple-element.518, f32[32,128]{1,0:T(8,128)S(1)} %get-tuple-element.519, ...), kind=kOutput, calls=%fused_computation.7.clone.1 | convolution fusion | flops 26251264 | bytes 295040 | tf_op jit(solution)/shard_map/while/body/eval_jaxpr/tab,tcb->tca/dot_general | solution.py:58
  320.9 3.3 fusion.96
  324.2 6.5 %fusion.97 = f32[32,3,128]{2,1,0:T(4,128)S(1)} fusion(f32[32]{0:T(128)S(1)} %dynamic-slice_bitcast_fusion.2, f32[32,128]{1,0:T(8,128)S(1)} %get-tuple-element.516, f32[32,128]{1,0:T(8,128)S(1)} %get-tuple-element.517, f32[32,128]{1,0:T(8,128)S(1)} %get-tuple-element.518, f32[32,128]{1,0:T(8,128)S(1)} %get-tuple-element.519, ...), kind=kOutput, calls=%fused_computation.7.clone.1 | convolution fusion | flops 26251264 | bytes 295040 | tf_op jit(solution)/shard_map/while/body/eval_jaxpr/tab,tcb->tca/dot_general | solution.py:58
  333.8 3.3 fusion.96
  337.1 6.5 %fusion.97 = f32[32,3,128]{2,1,0:T(4,128)S(1)} fusion(f32[32]{0:T(128)S(1)} %dynamic-slice_bitcast_fusion.2, f32[32,128]{1,0:T(8,128)S(1)} %get-tuple-element.516, f32[32,128]{1,0:T(8,128)S(1)} %get-tuple-element.517, f32[32,128]{1,0:T(8,128)S(1)} %get-tuple-element.518, f32[32,128]{1,0:T(8,128)S(1)} %get-tuple-element.519, ...), kind=kOutput, calls=%fused_computation.7.clone.1 | convolution fusion | flops 26251264 | bytes 295040 | tf_op jit(solution)/shard_map/while/body/eval_jaxpr/tab,tcb->tca/dot_general | solution.py:58
  346.7 3.3 fusion.96
  350.0 6.5 %fusion.97 = f32[32,3,128]{2,1,0:T(4,128)S(1)} fusion(f32[32]{0:T(128)S(1)} %dynamic-slice_bitcast_fusion.2, f32[32,128]{1,0:T(8,128)S(1)} %get-tuple-element.516, f32[32,128]{1,0:T(8,128)S(1)} %get-tuple-element.517, f32[32,128]{1,0:T(8,128)S(1)} %get-tuple-element.518, f32[32,128]{1,0:T(8,128)S(1)} %get-tuple-element.519, ...), kind=kOutput, calls=%fused_computation.7.clone.1 | convolution fusion | flops 26251264 | bytes 295040 | tf_op jit(solution)/shard_map/while/body/eval_jaxpr/tab,tcb->tca/dot_general | solution.py:58
  359.5 3.3 fusion.96
  362.8 6.5 %fusion.97 = f32[32,3,128]{2,1,0:T(4,128)S(1)} fusion(f32[32]{0:T(128)S(1)} %dynamic-slice_bitcast_fusion.2, f32[32,128]{1,0:T(8,128)S(1)} %get-tuple-element.516, f32[32,128]{1,0:T(8,128)S(1)} %get-tuple-element.517, f32[32,128]{1,0:T(8,128)S(1)} %get-tuple-element.518, f32[32,128]{1,0:T(8,128)S(1)} %get-tuple-element.519, ...), kind=kOutput, calls=%fused_computation.7.clone.1 | convolution fusion | flops 26251264 | bytes 295040 | tf_op jit(solution)/shard_map/while/body/eval_jaxpr/tab,tcb->tca/dot_general | solution.py:58
  372.4 3.3 fusion.96
  375.7 6.5 %fusion.97 = f32[32,3,128]{2,1,0:T(4,128)S(1)} fusion(f32[32]{0:T(128)S(1)} %dynamic-slice_bitcast_fusion.2, f32[32,128]{1,0:T(8,128)S(1)} %get-tuple-element.516, f32[32,128]{1,0:T(8,128)S(1)} %get-tuple-element.517, f32[32,128]{1,0:T(8,128)S(1)} %get-tuple-element.518, f32[32,128]{1,0:T(8,128)S(1)} %get-tuple-element.519, ...), kind=kOutput, calls=%fused_computation.7.clone.1 | convolution fusion | flops 26251264 | bytes 295040 | tf_op jit(solution)/shard_map/while/body/eval_jaxpr/tab,tcb->tca/dot_general | solution.py:58
  385.8 3.9 collective-permute-start.27
  (374 shorter events, 128.0 us)
Async XLA Ops:
  3.2 10.9 %copy-start.3 = (f32[3,8,8,128]{3,2,1,0:T(8,128)S(1)}, f32[3,8,8,128]{3,2,1,0:T(8,128)}, u32[]{:S(2)}) copy-start(f32[3,8,8,128]{3,2,1,0:T(8,128)} %param.39) | copy-start | bytes 294916
  3.2 12.9 %copy-start.2 = (f32[8,8,128]{2,1,0:T(8,128)S(1)}, f32[8,8,128]{2,1,0:T(8,128)}, u32[]{:S(2)}) copy-start(f32[8,8,128]{2,1,0:T(8,128)} %param.40) | copy-start | bytes 98308
  3.2 15.5 %copy-start = (f32[1,1,128,8,128]{4,3,2,1,0:T(8,128)S(1)}, f32[1,1,128,8,128]{4,3,2,1,0:T(8,128)}, u32[]{:S(2)}) copy-start(f32[1,1,128,8,128]{4,3,2,1,0:T(8,128)} %param.32) | copy-start | bytes 1572868
  3.2 15.5 %copy-start.9 = (s32[1,1,2,4]{3,2,1,0:T(2,128)S(1)}, s32[1,1,2,4]{3,2,1,0:T(2,128)}, u32[]{:S(2)}) copy-start(s32[1,1,2,4]{3,2,1,0:T(2,128)} %param.34) | copy-start | bytes 100
  3.3 15.6 %copy-start.6 = (s32[1,1,4,64]{3,2,1,0:T(4,128)S(1)}, s32[1,1,4,64]{3,2,1,0:T(4,128)}, u32[]{:S(2)}) copy-start(s32[1,1,4,64]{3,2,1,0:T(4,128)} %param.33) | copy-start | bytes 3076
  3.3 16.5 %copy-start.10 = (s32[4]{0:T(128)S(1)}, s32[4]{0:T(128)}, u32[]{:S(2)}) copy-start(s32[4]{0:T(128)} %constant.324.clone.1) | copy-start | bytes 52
  3.3 18.0 %copy-start.7 = (s32[1,1,384,4]{2,3,1,0:T(4,128)S(1)}, s32[1,1,384,4]{2,3,1,0:T(4,128)}, u32[]{:S(2)}) copy-start(s32[1,1,384,4]{2,3,1,0:T(4,128)} %param.37) | copy-start | bytes 18436
  4.2 40.0 %collective-permute-start.4 = (f32[1,64,8,128]{3,2,1,0:T(8,128)}, f32[1,64,8,128]{3,2,1,0:T(8,128)S(1)}, u32[]{:S(2)}, u32[]{:S(2)}) collective-permute-start(f32[1,64,8,128]{3,2,1,0:T(8,128)} %get-tuple-element.393), channel_id=1, source_target_pairs={{0,4},{4,8},{8,12},{12,16},{16,20},{20,24},{24,28},{1,5},{5,9},{9,... | collective-permute-start | bytes 786440 | tf_op jit(solution)/shard_map/ppermute | solution.py:21
  6.1 41.7 %collective-permute-start.5 = (f32[1,64,8,128]{3,2,1,0:T(8,128)}, f32[1,64,8,128]{3,2,1,0:T(8,128)S(1)}, u32[]{:S(2)}, u32[]{:S(2)}) collective-permute-start(f32[1,64,8,128]{3,2,1,0:T(8,128)} %get-tuple-element.392), channel_id=1, source_target_pairs={{4,0},{8,4},{12,8},{16,12},{20,16},{24,20},{28,24},{5,1},{9,5},{13... | collective-permute-start | bytes 786440 | tf_op jit(solution)/shard_map/ppermute | solution.py:24
  10.6 37.1 %collective-permute-start.6 = (f32[1,64,8,128]{3,2,1,0:T(8,128)S(1)}, f32[1,64,8,128]{3,2,1,0:T(8,128)S(1)}, u32[]{:S(2)}, u32[]{:S(2)}) collective-permute-start(f32[1,64,8,128]{3,2,1,0:T(8,128)S(1)} %get-tuple-element.391), channel_id=1, source_target_pairs={{0,1},{1,2},{2,3},{4,5},{5,6},{6,7},{8,9},{9,10},{10,11},{12,13},{... | collective-permute-start | bytes 786440 | tf_op jit(solution)/shard_map/ppermute | solution.py:21
  14.2 16.9 %collective-permute-start.8 = (f32[3,1,8,128]{3,2,1,0:T(8,128)S(1)}, f32[3,1,8,128]{3,2,1,0:T(8,128)S(1)}, u32[]{:S(2)}, u32[]{:S(2)}) collective-permute-start(f32[3,1,8,128]{3,2,1,0:T(8,128)S(1)} %get-tuple-element.401), channel_id=1, source_target_pairs={{0,4},{4,8},{8,12},{12,16},{16,20},{20,24},{24,28},{1,5},{5,9},{9,... | collective-permute-start | bytes 36872 | tf_op jit(solution)/shard_map/ppermute | solution.py:21
  16.1 5.8 %collective-permute-start.1 = (f32[1,8,128]{2,1,0:T(8,128)S(1)}, f32[1,8,128]{2,1,0:T(8,128)S(1)}, u32[]{:S(2)}, u32[]{:S(2)}) collective-permute-start(f32[1,8,128]{2,1,0:T(8,128)S(1)} %get-tuple-element.417), channel_id=1, source_target_pairs={{0,4},{4,8},{8,12},{12,16},{16,20},{20,24},{24,28},{1,5},{5,9},{9,... | collective-permute-start | bytes 12296 | tf_op jit(solution)/shard_map/ppermute | solution.py:21
  21.9 4.6 %collective-permute-start = (f32[1,8,128]{2,1,0:T(8,128)S(1)}, f32[1,8,128]{2,1,0:T(8,128)S(1)}, u32[]{:S(2)}, u32[]{:S(2)}) collective-permute-start(f32[1,8,128]{2,1,0:T(8,128)S(1)} %get-tuple-element.416), channel_id=1, source_target_pairs={{4,0},{8,4},{12,8},{16,12},{20,16},{24,20},{28,24},{5,1},{9,5},{13... | collective-permute-start | bytes 12296 | tf_op jit(solution)/shard_map/ppermute | solution.py:24
  26.5 5.9 %collective-permute-start.9 = (f32[3,1,8,128]{3,2,1,0:T(8,128)S(1)}, f32[3,1,8,128]{3,2,1,0:T(8,128)S(1)}, u32[]{:S(2)}, u32[]{:S(2)}) collective-permute-start(f32[3,1,8,128]{3,2,1,0:T(8,128)S(1)} %get-tuple-element.400), channel_id=1, source_target_pairs={{4,0},{8,4},{12,8},{16,12},{20,16},{24,20},{28,24},{5,1},{9,5},{13... | collective-permute-start | bytes 36872 | tf_op jit(solution)/shard_map/ppermute | solution.py:24
  32.4 5.9 %collective-permute-start.10 = (f32[3,10,1,128]{3,2,1,0:T(1,128)S(1)}, f32[3,10,1,128]{3,2,1,0:T(1,128)S(1)}, u32[]{:S(2)}, u32[]{:S(2)}) collective-permute-start(f32[3,10,1,128]{3,2,1,0:T(1,128)S(1)} %get-tuple-element.398), channel_id=1, source_target_pairs={{0,1},{1,2},{2,3},{4,5},{5,6},{6,7},{8,9},{9,10},{10,11},{12,13},{... | collective-permute-start | bytes 46088 | tf_op jit(solution)/shard_map/ppermute | solution.py:21
  35.9 5.8 %collective-permute-start.11 = (f32[3,10,1,128]{3,2,1,0:T(1,128)S(1)}, f32[3,10,1,128]{3,2,1,0:T(1,128)S(1)}, u32[]{:S(2)}, u32[]{:S(2)}) collective-permute-start(f32[3,10,1,128]{3,2,1,0:T(1,128)S(1)} %get-tuple-element.399), channel_id=1, source_target_pairs={{1,0},{2,1},{3,2},{5,4},{6,5},{7,6},{9,8},{10,9},{11,10},{13,12},{... | collective-permute-start | bytes 46088 | tf_op jit(solution)/shard_map/ppermute | solution.py:24
  38.3 9.5 %collective-permute-start.7 = (f32[1,64,8,128]{3,2,1,0:T(8,128)S(1)}, f32[1,64,8,128]{3,2,1,0:T(8,128)S(1)}, u32[]{:S(2)}, u32[]{:S(2)}) collective-permute-start(f32[1,64,8,128]{3,2,1,0:T(8,128)S(1)} %get-tuple-element.390), channel_id=1, source_target_pairs={{1,0},{2,1},{3,2},{5,4},{6,5},{7,6},{9,8},{10,9},{11,10},{13,12},{... | collective-permute-start | bytes 786440 | tf_op jit(solution)/shard_map/ppermute | solution.py:24
  41.7 86.2 %collective-permute-start.2 = (f32[10,1,128]{2,1,0:T(1,128)S(1)}, f32[10,1,128]{2,1,0:T(1,128)S(1)}, u32[]{:S(2)}, u32[]{:S(2)}) collective-permute-start(f32[10,1,128]{2,1,0:T(1,128)S(1)} %get-tuple-element.409), channel_id=1, source_target_pairs={{1,0},{2,1},{3,2},{5,4},{6,5},{7,6},{9,8},{10,9},{11,10},{13,12},{... | collective-permute-start | bytes 15368 | tf_op jit(solution)/shard_map/ppermute | solution.py:24
  44.1 83.8 %collective-permute-start.3 = (f32[10,1,128]{2,1,0:T(1,128)S(1)}, f32[10,1,128]{2,1,0:T(1,128)S(1)}, u32[]{:S(2)}, u32[]{:S(2)}) collective-permute-start(f32[10,1,128]{2,1,0:T(1,128)S(1)} %get-tuple-element.408), channel_id=1, source_target_pairs={{0,1},{1,2},{2,3},{4,5},{5,6},{6,7},{8,9},{9,10},{10,11},{12,13},{... | collective-permute-start | bytes 15368 | tf_op jit(solution)/shard_map/ppermute | solution.py:21
  121.3 18.3 %copy-start.1 = (f32[8,8,128]{2,1,0:T(8,128)S(1)}, f32[8,8,128]{2,1,0:T(8,128)}, u32[]{:S(2)}) copy-start(f32[8,8,128]{2,1,0:T(8,128)} %param.43) | copy-start | bytes 98308
  121.3 18.3 %copy-start.4 = (f32[8,8,128]{2,1,0:T(8,128)S(1)}, f32[8,8,128]{2,1,0:T(8,128)}, u32[]{:S(2)}) copy-start(f32[8,8,128]{2,1,0:T(8,128)} %param.41) | copy-start | bytes 98308
  121.4 18.3 %copy-start.5 = (f32[8,8,128]{2,1,0:T(8,128)S(1)}, f32[8,8,128]{2,1,0:T(8,128)}, u32[]{:S(2)}) copy-start(f32[8,8,128]{2,1,0:T(8,128)} %param.42) | copy-start | bytes 98308
  121.4 50.2 %copy-start.8 = (s32[1,1,512,2]{2,3,1,0:T(2,128)S(1)}, s32[1,1,512,2]{2,3,1,0:T(2,128)}, u32[]{:S(2)}) copy-start(s32[1,1,512,2]{2,3,1,0:T(2,128)} %param.35) | copy-start | bytes 12292
  121.5 6.7 %collective-permute-start.12 = (f32[4,1,10,128]{3,0,2,1:T(4,128)S(1)}, f32[4,1,10,128]{3,0,2,1:T(4,128)S(1)}, u32[]{:S(2)}, u32[]{:S(2)}) collective-permute-start(f32[4,1,10,128]{3,0,2,1:T(4,128)S(1)} %get-tuple-element.397), channel_id=1, source_target_pairs={{0,4},{4,8},{8,12},{12,16},{16,20},{20,24},{24,28},{1,5},{5,9},{9,... | collective-permute-start | bytes 61448 | tf_op jit(solution)/shard_map/ppermute | solution.py:21
  123.4 6.0 %collective-permute-start.13 = (f32[4,1,10,128]{3,0,2,1:T(4,128)S(1)}, f32[4,1,10,128]{3,0,2,1:T(4,128)S(1)}, u32[]{:S(2)}, u32[]{:S(2)}) collective-permute-start(f32[4,1,10,128]{3,0,2,1:T(4,128)S(1)} %get-tuple-element.396), channel_id=1, source_target_pairs={{4,0},{8,4},{12,8},{16,12},{20,16},{24,20},{28,24},{5,1},{9,5},{13... | collective-permute-start | bytes 61448 | tf_op jit(solution)/shard_map/ppermute | solution.py:24
  129.4 5.9 %collective-permute-start.14 = (f32[4,12,1,128]{3,0,2,1:T(4,128)S(1)}, f32[4,12,1,128]{3,0,2,1:T(4,128)S(1)}, u32[]{:S(2)}, u32[]{:S(2)}) collective-permute-start(f32[4,12,1,128]{3,0,2,1:T(4,128)S(1)} %get-tuple-element.395), channel_id=1, source_target_pairs={{0,1},{1,2},{2,3},{4,5},{5,6},{6,7},{8,9},{9,10},{10,11},{12,13},{... | collective-permute-start | bytes 73736 | tf_op jit(solution)/shard_map/ppermute | solution.py:21
  131.9 5.7 %collective-permute-start.15 = (f32[4,12,1,128]{3,0,2,1:T(4,128)S(1)}, f32[4,12,1,128]{3,0,2,1:T(4,128)S(1)}, u32[]{:S(2)}, u32[]{:S(2)}) collective-permute-start(f32[4,12,1,128]{3,0,2,1:T(4,128)S(1)} %get-tuple-element.394), channel_id=1, source_target_pairs={{1,0},{2,1},{3,2},{5,4},{6,5},{7,6},{9,8},{10,9},{11,10},{13,12},{... | collective-permute-start | bytes 73736 | tf_op jit(solution)/shard_map/ppermute | solution.py:24
  139.8 5.0 %collective-permute-start.16 = (f32[1,8,128]{2,1,0:T(8,128)S(1)}, f32[1,8,128]{2,1,0:T(8,128)S(1)}, u32[]{:S(2)}, u32[]{:S(2)}) collective-permute-start(f32[1,8,128]{2,1,0:T(8,128)S(1)} %get-tuple-element.415), channel_id=1, source_target_pairs={{4,0},{8,4},{12,8},{16,12},{20,16},{24,20},{28,24},{5,1},{9,5},{13... | collective-permute-start | bytes 12296 | tf_op jit(solution)/shard_map/ppermute | solution.py:24
  142.9 5.8 %collective-permute-start.17 = (f32[1,8,128]{2,1,0:T(8,128)S(1)}, f32[1,8,128]{2,1,0:T(8,128)S(1)}, u32[]{:S(2)}, u32[]{:S(2)}) collective-permute-start(f32[1,8,128]{2,1,0:T(8,128)S(1)} %get-tuple-element.414), channel_id=1, source_target_pairs={{0,4},{4,8},{8,12},{12,16},{16,20},{20,24},{24,28},{1,5},{5,9},{9,... | collective-permute-start | bytes 12296 | tf_op jit(solution)/shard_map/ppermute | solution.py:21
  148.7 5.9 %collective-permute-start.18 = (f32[10,1,128]{2,1,0:T(1,128)S(1)}, f32[10,1,128]{2,1,0:T(1,128)S(1)}, u32[]{:S(2)}, u32[]{:S(2)}) collective-permute-start(f32[10,1,128]{2,1,0:T(1,128)S(1)} %get-tuple-element.407), channel_id=1, source_target_pairs={{1,0},{2,1},{3,2},{5,4},{6,5},{7,6},{9,8},{10,9},{11,10},{13,12},{... | collective-permute-start | bytes 15368 | tf_op jit(solution)/shard_map/ppermute | solution.py:24
  152.1 5.5 %collective-permute-start.19 = (f32[10,1,128]{2,1,0:T(1,128)S(1)}, f32[10,1,128]{2,1,0:T(1,128)S(1)}, u32[]{:S(2)}, u32[]{:S(2)}) collective-permute-start(f32[10,1,128]{2,1,0:T(1,128)S(1)} %get-tuple-element.406), channel_id=1, source_target_pairs={{0,1},{1,2},{2,3},{4,5},{5,6},{6,7},{8,9},{9,10},{10,11},{12,13},{... | collective-permute-start | bytes 15368 | tf_op jit(solution)/shard_map/ppermute | solution.py:21
  157.9 5.0 %collective-permute-start.20 = (f32[1,8,128]{2,1,0:T(8,128)S(1)}, f32[1,8,128]{2,1,0:T(8,128)S(1)}, u32[]{:S(2)}, u32[]{:S(2)}) collective-permute-start(f32[1,8,128]{2,1,0:T(8,128)S(1)} %get-tuple-element.413), channel_id=1, source_target_pairs={{4,0},{8,4},{12,8},{16,12},{20,16},{24,20},{28,24},{5,1},{9,5},{13... | collective-permute-start | bytes 12296 | tf_op jit(solution)/shard_map/ppermute | solution.py:24
  159.8 5.8 %collective-permute-start.21 = (f32[1,8,128]{2,1,0:T(8,128)S(1)}, f32[1,8,128]{2,1,0:T(8,128)S(1)}, u32[]{:S(2)}, u32[]{:S(2)}) collective-permute-start(f32[1,8,128]{2,1,0:T(8,128)S(1)} %get-tuple-element.412), channel_id=1, source_target_pairs={{0,4},{4,8},{8,12},{12,16},{16,20},{20,24},{24,28},{1,5},{5,9},{9,... | collective-permute-start | bytes 12296 | tf_op jit(solution)/shard_map/ppermute | solution.py:21
  165.7 6.3 %collective-permute-start.22 = (f32[10,1,128]{2,1,0:T(1,128)S(1)}, f32[10,1,128]{2,1,0:T(1,128)S(1)}, u32[]{:S(2)}, u32[]{:S(2)}) collective-permute-start(f32[10,1,128]{2,1,0:T(1,128)S(1)} %get-tuple-element.405), channel_id=1, source_target_pairs={{1,0},{2,1},{3,2},{5,4},{6,5},{7,6},{9,8},{10,9},{11,10},{13,12},{... | collective-permute-start | bytes 15368 | tf_op jit(solution)/shard_map/ppermute | solution.py:24
  167.6 5.5 %collective-permute-start.23 = (f32[10,1,128]{2,1,0:T(1,128)S(1)}, f32[10,1,128]{2,1,0:T(1,128)S(1)}, u32[]{:S(2)}, u32[]{:S(2)}) collective-permute-start(f32[10,1,128]{2,1,0:T(1,128)S(1)} %get-tuple-element.404), channel_id=1, source_target_pairs={{0,1},{1,2},{2,3},{4,5},{5,6},{6,7},{8,9},{9,10},{10,11},{12,13},{... | collective-permute-start | bytes 15368 | tf_op jit(solution)/shard_map/ppermute | solution.py:21
  173.4 210.5 %collective-permute-start.24 = (f32[1,8,128]{2,1,0:T(8,128)S(1)}, f32[1,8,128]{2,1,0:T(8,128)S(1)}, u32[]{:S(2)}, u32[]{:S(2)}) collective-permute-start(f32[1,8,128]{2,1,0:T(8,128)S(1)} %get-tuple-element.411), channel_id=1, source_target_pairs={{4,0},{8,4},{12,8},{16,12},{20,16},{24,20},{28,24},{5,1},{9,5},{13... | collective-permute-start | bytes 12296 | tf_op jit(solution)/shard_map/ppermute | solution.py:24
  175.3 208.6 %collective-permute-start.25 = (f32[1,8,128]{2,1,0:T(8,128)S(1)}, f32[1,8,128]{2,1,0:T(8,128)S(1)}, u32[]{:S(2)}, u32[]{:S(2)}) collective-permute-start(f32[1,8,128]{2,1,0:T(8,128)S(1)} %get-tuple-element.410), channel_id=1, source_target_pairs={{0,4},{4,8},{8,12},{12,16},{16,20},{20,24},{24,28},{1,5},{5,9},{9,... | collective-permute-start | bytes 12296 | tf_op jit(solution)/shard_map/ppermute | solution.py:21
  383.9 8.5 %collective-permute-start.26 = (f32[10,1,128]{2,1,0:T(1,128)S(1)}, f32[10,1,128]{2,1,0:T(1,128)S(1)}, u32[]{:S(2)}, u32[]{:S(2)}) collective-permute-start(f32[10,1,128]{2,1,0:T(1,128)S(1)} %get-tuple-element.403), channel_id=1, source_target_pairs={{1,0},{2,1},{3,2},{5,4},{6,5},{7,6},{9,8},{10,9},{11,10},{13,12},{... | collective-permute-start | bytes 15368 | tf_op jit(solution)/shard_map/ppermute | solution.py:24
  385.8 6.5 %collective-permute-start.27 = (f32[10,1,128]{2,1,0:T(1,128)S(1)}, f32[10,1,128]{2,1,0:T(1,128)S(1)}, u32[]{:S(2)}, u32[]{:S(2)}) collective-permute-start(f32[10,1,128]{2,1,0:T(1,128)S(1)} %get-tuple-element.402), channel_id=1, source_target_pairs={{0,1},{1,2},{2,3},{4,5},{5,6},{6,7},{8,9},{9,10},{10,11},{12,13},{... | collective-permute-start | bytes 15368 | tf_op jit(solution)/shard_map/ppermute | solution.py:21
where the time goes:
time: 396 us; the launch traced here: 393 us
  matrix products  150 us (38%)
  other arithmetic  101 us (26%)
  starting transfers between devices  79.3 us (20%)
  local copies, waits for them, and re-layouts  40.4 us (10%)
  waiting for transfers between devices  19.1 us (5%)
    dot_general x16, matrix products, tile_step(): jnp.einsum('tab,tcb->tca', weight, second_side[:, 0:3, :], precision=topm...  104 us
    reduce_sum x16, other arithmetic, tile_step(): pushed = first_side[:, 0:3, :] * jnp.sum(weight, axis=2)[:, None, :]  52.2 us
    ppermute x14, starting transfers between devices, extended_2(): lax.ppermute(lax.slice_in_dim(block, 0, width, axis=dim), axis, backward)  40.9 us
    ppermute x14, starting transfers between devices, extended_2(): lax.ppermute(lax.slice_in_dim(block, block.shape[dim] - width, None, axis...  38.4 us
    scatter-add x16, other arithmetic, tile_step(): force_total.at[pair_group[:, 0]].add(stiffness * (pushed - pulled))  26.4 us
    dot_general x6, matrix products, group_advance(): jnp.einsum('gkcz,gpz->gkcp', local_flow, depth_pick, precision=topmost_va...  24.8 us
    dot_general x6, matrix products, group_advance(): jnp.einsum('gkcp,gpz->gkcz', slot_breakdown, depth_pick, precision=topmos...  18 us
    ppermute x14, waiting for transfers between devices, extended_2(): lax.ppermute(lax.slice_in_dim(block, block.shape[dim] - width, None, axis...  11.4 us
  transfers between devices with their start and end apart: 28, of which 10 were waited for; matrix products, arithmetic and copies ran while one was open for 72% of the time, Pallas kernels for 0%

commit v1 on v0

v1 whole, which is shorter than its diff:
```python
import functools

import jax
import jax.numpy as jnp
from jax import lax
from jax.experimental import pallas as pl
from jax.experimental.pallas import tpu as pltpu
from jax.sharding import PartitionSpec as P

ITERS = 4
MOVERS = 16
WIDE = ITERS
UNROLL = 8
MESH = pl.DeviceIdType.MESH
AROUND = [(dx, dy) for dx in (-1, 0, 1) for dy in (-1, 0, 1) if (dx, dy) != (0, 0)]
GROUPS = [(1, 0), (-1, 0), (0, 1), (0, -1)]
f32, bf16 = jnp.float32, jnp.bfloat16
VM = pltpu.VMEM
LIMIT = 48 * 1024 * 1024


def span(step, count, width):
    if step == 0:
        return 0, count
    return (count - width, width) if step > 0 else (0, width)


def place(step, count, width):
    if step == 0:
        return width, count
    return (width + count, width) if step > 0 else (0, width)


def neighbour(step, n_x, n_y):
    a, b = lax.axis_index("gx") + step[0], lax.axis_index("gy") + step[1]
    return (a >= 0) & (a < n_x) & (b >= 0) & (b < n_y), (a, b)


def enter(n_x, n_y):
    barrier = pltpu.get_barrier_semaphore()
    for step in AROUND:
        there, device = neighbour(step, n_x, n_y)

        @pl.when(there)
        def _():
            pl.semaphore_signal(barrier, inc=1, device_id=device, device_id_type=MESH)

    peers = 0
    for step in AROUND:
        there, device = neighbour(step, n_x, n_y)
        peers = peers + there.astype(jnp.int32)
    pl.semaphore_wait(barrier, peers)


def pick_kernel(send_ref, own_ref, out_ref):
    total = out_ref.shape[0]

    def step(s, carry):
        for u in range(8):
            out_ref[s * 8 + u] = own_ref[send_ref[s * 8 + u]]
        return carry

    lax.fori_loop(0, total // 8, step, 0)


def exchange_kernel(n_x, n_y, blocks, flow, press, screen, source, solid,
                    got, columns, p_ext, g_ext, s_ext, *scratch):
    n = len(AROUND)
    wide_out, wide_in = scratch[0:n], scratch[n:2 * n]
    slim_out, slim_in = scratch[2 * n:3 * n], scratch[3 * n:4 * n]
    sends, recvs = scratch[4 * n:]
    cx, cy = press.shape[0], press.shape[1]
    enter(n_x, n_y)

    def block_copy(d):
        there, device = neighbour(GROUPS[d], n_x, n_y)
        return there, pltpu.make_async_remote_copy(
            src_ref=blocks.at[d], dst_ref=got.at[d], send_sem=sends.at[2 * n + d],
            recv_sem=recvs.at[2 * n + d], device_id=device, device_id_type=MESH)

    for d in (2, 3, 0, 1):
        there, copy = block_copy(d)

        @pl.when(there)
        def _():
            copy.start()

    gain = 1.0 / (6.0 + screen[...])
    rest = source[...] - 2.0 * solid[...]
    g_ext[...] = jnp.zeros(g_ext.shape, f32)
    s_ext[...] = jnp.zeros(s_ext.shape, f32)
    p_ext[...] = jnp.zeros(p_ext.shape, f32)
    g_ext[WIDE:WIDE + cx, WIDE:WIDE + cy, :] = gain
    s_ext[WIDE:WIDE + cx, WIDE:WIDE + cy, :] = rest
    p_ext[WIDE:WIDE + cx, WIDE:WIDE + cy, :] = press[...]

    def halo_copies(e):
        there, device = neighbour(AROUND[e], n_x, n_y)
        back = AROUND.index((-AROUND[e][0], -AROUND[e][1]))
        kw = dict(device_id=device, device_id_type=MESH)
        return there, [
            pltpu.make_async_remote_copy(src_ref=wide_out[e], dst_ref=wide_in[back],
                                         send_sem=sends.at[e], recv_sem=recvs.at[back], **kw),
            pltpu.make_async_remote_copy(src_ref=slim_out[e], dst_ref=slim_in[back],
                                         send_sem=sends.at[n + e], recv_sem=recvs.at[n + back],
                                         **kw)]

    for e, (dx, dy) in enumerate(AROUND):
        x0, xn = span(dx, cx, WIDE)
        y0, yn = span(dy, cy, WIDE)
        wide_out[e][0] = press[x0:x0 + xn, y0:y0 + yn, :]
        wide_out[e][1] = gain[x0:x0 + xn, y0:y0 + yn, :]
        wide_out[e][2] = rest[x0:x0 + xn, y0:y0 + yn, :]
        x0, xn = span(dx, cx, 1)
        y0, yn = span(dy, cy, 1)
        for c in range(3):
            if dx and dy:
                slim_out[e][c:c + 1, :] = flow[c, x0, y0:y0 + 1, :]
            elif dx:
                slim_out[e][c] = flow[c, x0]
            else:
                for x in range(cx):
                    slim_out[e][c, x:x + 1, :] = flow[c, x, y0:y0 + 1, :]
        there, copies = halo_copies(e)

        @pl.when(there)
        def _():
            for copy in copies:
                copy.start()

    columns[...] = jnp.zeros(columns.shape, f32)
    for c in range(3):
        for x in range(cx):
            first = ((x + 1) * (cy + 2) + 1) * 8 + c
            columns[pl.ds(first, cy, stride=8), :] = flow[c, x]

    for d in range(4):
        there, copy = block_copy(d)
        back = (-GROUPS[d][0], -GROUPS[d][1])
        fed, unused = neighbour(back, n_x, n_y)

        @pl.when(jnp.logical_not(fed))
        def _():
            got[d] = jnp.zeros(got.shape[1:], f32)

    for e, (dx, dy) in enumerate(AROUND):
        there, copies = halo_copies(e)
        back = AROUND.index((-dx, -dy))

        @pl.when(there)
        def _():
            here, from_it = halo_copies(back)
            for copy in from_it:
                copy.wait_recv()
            x0, xn = place(dx, cx, WIDE)
            y0, yn = place(dy, cy, WIDE)
            p_ext[x0:x0 + xn, y0:y0 + yn, :] = wide_in[e][0]
            g_ext[x0:x0 + xn, y0:y0 + yn, :] = wide_in[e][1]
            s_ext[x0:x0 + xn, y0:y0 + yn, :] = wide_in[e][2]
            x0, xn = place(dx, cx, 1)
            y0, yn = place(dy, cy, 1)
            for c in range(3):
                if dx and dy:
                    columns[pl.ds((x0 * (cy + 2) + y0) * 8 + c, 1), :] = slim_in[e][c:c + 1, :]
                elif dx:
                    first = (x0 * (cy + 2) + 1) * 8 + c
                    columns[pl.ds(first, cy, stride=8), :] = slim_in[e][c]
                else:
                    first = ((cy + 2) + y0) * 8 + c
                    columns[pl.ds(first, cx, stride=8 * (cy + 2)), :] = slim_in[e][c]
            for copy in copies:
                copy.wait_send()

    for d in range(4):
        there, copy = block_copy(d)
        fed, unused = neighbour((-GROUPS[d][0], -GROUPS[d][1]), n_x, n_y)

        @pl.when(fed)
        def _():
            copy.wait_recv()

        @pl.when(there)
        def _():
            copy.wait_send()


def split3(value):
    high = value.astype(bf16).astype(f32)
    rest = value - high
    mid = rest.astype(bf16).astype(f32)
    return high, mid, (rest - mid).astype(bf16).astype(f32)


def forces_kernel(pairs, count, tiles, send, moves, own, got, cells, columns,
                  deposit, force, owned, tab_a, tab_b, tab_y, total, drag, dep):
    n_own, slots = own.shape[0], got.shape[1]
    pool = n_own + 4 * slots
    cx, cy = deposit.shape[1], deposit.shape[2]
    depth = cells.shape[1]
    row = lax.broadcasted_iota(jnp.int32, (8, depth), 0)
    low = row < 4
    deep = lax.broadcasted_iota(jnp.int32, (depth, depth), 0)

    def mark(k, carry):
        owned[k] = 1.0
        return carry

    lax.fori_loop(0, n_own, mark, 0)
    for d in range(4):
        def unmark(s, carry):
            owned[send[d * slots + s]] = 0.0
            return carry

        lax.fori_loop(0, moves[d], unmark, 0)
    dep[...] = jnp.zeros(dep.shape, f32)
    total[...] = jnp.zeros(total.shape, f32)

    def tables(m, block):
        both = jnp.where(low, block, pltpu.roll(block, 4, 0))
        c1, c2, c3 = split3(both)
        square = jnp.where(row < 3, -both * both, jnp.where(row == 3, both * both, 0.0))
        n1, n2, n3 = split3(jnp.sum(square, axis=0, keepdims=True))
        ones = jnp.ones((8, depth), f32)
        zeros = jnp.zeros((8, depth), f32)
        a3 = jnp.where(row == 0, n1, jnp.where(row == 1, n2, jnp.where(row == 2, n3, jnp.where(row < 6, ones, zeros))))
        b3 = jnp.where(row == 3, n1, jnp.where(row == 4, n2, jnp.where(row == 5, n3, jnp.where(row < 3, ones, zeros))))
        a = jnp.concatenate([c1, c2, jnp.where(low, c1, c3), a3], axis=0)
        twice = 2.0 * jnp.where(low, c1, c2)
        b = jnp.concatenate([twice, twice, 2.0 * jnp.where(low, c3, c1), b3], axis=0)
        third = jnp.where(row == 3, ones, zeros)
        r1, r2, r3 = c1[3:4], c2[3:4], c3[3:4]
        reach = jnp.where(row == 3, r1, jnp.where(row == 4, r2, jnp.where(row == 5, r3, zeros)))
        r = jnp.concatenate([third, third, jnp.where(row == 7, ones, zeros), reach], axis=0)
        y1 = jnp.where(row < 3, c1, jnp.where(row == 3, ones, jnp.where(row < 7, c2, zeros)))
        y2 = jnp.where(row < 3, c1, jnp.where(row == 3, ones, zeros))
        y = jnp.concatenate([jnp.concatenate([y1, y2], axis=1),
                             jnp.zeros((8, 2 * depth), f32)], axis=0)
        tab_a[m] = a.astype(bf16)
        tab_b[m] = jnp.concatenate([b, r], axis=1).astype(bf16)
        tab_y[m] = y.astype(bf16)

    def drag_block(m, block, cell, mine):
        slot = cell // depth
        z = cell - slot * depth
        index = jnp.broadcast_to(z, (8, depth))
        slot8 = jnp.broadcast_to(slot, (8, depth))
        fluid = jnp.zeros((8, depth), f32)
        where = [pl.multiple_of(tiles[m * 4 + k] * 8, 8) for k in range(4)]
        for k in range(4):
            at = jnp.take_along_axis(columns[pl.ds(where[k], 8), :], index, axis=1)
            fluid = jnp.where(slot8 == k, at, fluid)
        pull = block[7:8, :] * (fluid - pltpu.roll(block, 4, 0))
        load = jnp.where(row < 3, pull, jnp.where(low, block * block * block, 0.0)) * mine
        drag[m] = load
        high = load.astype(bf16).astype(f32)
        parts = jnp.where(low, high, pltpu.roll(load - high, 4, 0))
        left = jnp.concatenate([jnp.where(slot8 == k, parts, 0.0) for k in range(4)], axis=0)
        hot = jnp.where(deep == z, 1.0, 0.0).astype(bf16)
        out = lax.dot_general(left.astype(bf16), hot, (((1,), (1,)), ((), ())),
                              preferred_element_type=f32)
        return where, out

    def deposit_all(results):
        for where, out in results:
            for k in range(4):
                dep[pl.ds(where[k], 8), :] += out[8 * k:8 * k + 8]

    def own_step(s, carry):
        cell8 = cells[pl.ds(pl.multiple_of(s * 8, 8), 8), :]
        results = []
        for u in range(8):
            m = s * 8 + u
            block = own[m]
            tables(m, block)
            results.append(drag_block(m, block, cell8[u:u + 1], owned[m]))
        deposit_all(results)
        return carry

    lax.fori_loop(0, n_own // 8, own_step, 0)
    for d in range(4):
        def got_step(s, carry):
            base = n_own + d * slots
            cell8 = cells[pl.ds(pl.multiple_of(base + s * 8, 8), 8), :]
            results = []
            for u in range(8):
                k = s * 8 + u
                mine = jnp.where(k < moves[4 + d], 1.0, 0.0).astype(f32)
                results.append(drag_block(base + k, got[d, k], cell8[u:u + 1], mine))
            deposit_all(results)
            return carry

        lax.fori_loop(0, MOVERS // 8, got_step, 0)

        def table_step(s, carry):
            for u in range(8):
                tables(n_own + d * slots + s * 8 + u, got[d, s * 8 + u])
            return carry

        lax.fori_loop(0, slots // 8, table_step, 0)

    for c in range(4):
        for x in range(cx):
            high = dep[pl.ds(x * cy * 8 + c, cy, stride=8), :]
            rest = dep[pl.ds(x * cy * 8 + 4 + c, cy, stride=8), :]
            deposit[c, x] = high + rest

    def tile_step(s, carry):
        results = []
        for u in range(UNROLL):
            t = s * UNROLL + u
            i, j = pairs[2 * t], pairs[2 * t + 1]
            mr = lax.dot_general(tab_a[j], tab_b[i], (((0,), (0,)), ((), ())),
                                 preferred_element_type=f32)
            over, reach = mr[:, :depth], mr[:, depth:]
            inverse = pl.reciprocal(reach, approx=True)
            inverse = inverse * (2.0 - reach * inverse)
            weight = jnp.maximum(over, 0.0) * (inverse * inverse)
            w1 = weight.astype(bf16)
            w2 = (weight - w1.astype(f32)).astype(bf16)
            out = lax.dot_general(tab_y[j], jnp.concatenate([w1, w2], axis=0),
                                  (((1,), (0,)), ((), ())), preferred_element_type=f32)
            keep = jnp.where(t < count[0], 1.0, 0.0).astype(f32)
            results.append((i, out[0:8] * keep))
        for i, out in results:
            total[i] += out
        return carry

    lax.fori_loop(0, (count[0] + UNROLL - 1) // UNROLL, tile_step, 0)

    def finish(m, block):
        sums = total[m]
        sums = sums + pltpu.roll(sums, 4, 0)
        contact = 0.5 * (block * sums[3:4] - sums)
        force[m] = (contact + drag[m])[0:3]

    def own_finish(s, carry):
        for u in range(8):
            finish(s * 8 + u, own[s * 8 + u])
        return carry

    lax.fori_loop(0, n_own // 8, own_finish, 0)
    for d in range(4):
        def got_finish(s, carry):
            for u in range(8):
                finish(n_own + d * slots + s * 8 + u, got[d, s * 8 + u])
            return carry

        lax.fori_loop(0, MOVERS // 8, got_finish, 0)
        force[pl.ds(n_own + d * slots + MOVERS, slots - MOVERS)] = jnp.zeros(
            (slots - MOVERS, 3, depth), f32)


def pressure_kernel(n_x, n_y, deposit, p_ext, g_ext, s_ext, press, drag_sum, load, *scratch):
    n = len(AROUND)
    wide_out, wide_in = scratch[0:n], scratch[n:2 * n]
    slim_out, slim_in = scratch[2 * n:3 * n], scratch[3 * n:4 * n]
    sends, recvs = scratch[4 * n:]
    cx, cy = press.shape[0], press.shape[1]

    def copies_of(e):
        there, device = neighbour(AROUND[e], n_x, n_y)
        back = AROUND.index((-AROUND[e][0], -AROUND[e][1]))
        kw = dict(device_id=device, device_id_type=MESH)
        return there, [
            pltpu.make_async_remote_copy(src_ref=wide_out[e], dst_ref=wide_in[back],
                                         send_sem=sends.at[e], recv_sem=recvs.at[back], **kw),
            pltpu.make_async_remote_copy(src_ref=slim_out[e], dst_ref=slim_in[back],
                                         send_sem=sends.at[n + e], recv_sem=recvs.at[n + back],
                                         **kw)]

    for e, (dx, dy) in enumerate(AROUND):
        x0, xn = span(dx, cx + 2, WIDE)
        y0, yn = span(dy, cy + 2, WIDE)
        wide_out[e][...] = deposit[3, x0:x0 + xn, y0:y0 + yn, :]
        x0 = cx + 1 if dx > 0 else 0
        y0 = cy + 1 if dy > 0 else 0
        for c in range(3):
            if dx and dy:
                slim_out[e][c:c + 1, :] = deposit[c, x0, y0:y0 + 1, :]
            elif dx:
                slim_out[e][c] = deposit[c, x0, 1:1 + cy, :]
            else:
                for x in range(cx):
                    slim_out[e][c, x:x + 1, :] = deposit[c, x + 1, y0:y0 + 1, :]
    enter(n_x, n_y)
    for e in range(n):
        there, copies = copies_of(e)

        @pl.when(there)
        def _():
            for copy in copies:
                copy.start()

    load[...] = jnp.zeros(load.shape, f32)
    load[WIDE - 1:WIDE + cx + 1, WIDE - 1:WIDE + cy + 1, :] = deposit[3]
    drag_sum[...] = deposit[0:3, 1:1 + cx, 1:1 + cy, :]

    def put(step, count):
        if step == 0:
            return WIDE - 1, count + 2
        return (WIDE + count - 1, WIDE) if step > 0 else (1, WIDE)

    for e, (dx, dy) in enumerate(AROUND):
        there, copies = copies_of(e)
        back = AROUND.index((-dx, -dy))

        @pl.when(there)
        def _():
            here, from_it = copies_of(back)
            for copy in from_it:
                copy.wait_recv()
            x0, xn = put(dx, cx)
            y0, yn = put(dy, cy)
            load[x0:x0 + xn, y0:y0 + yn, :] += wide_in[e][...]
            x0 = cx - 1 if dx > 0 else 0
            y0 = cy - 1 if dy > 0 else 0
            for c in range(3):
                if dx and dy:
                    drag_sum[c, x0, y0:y0 + 1, :] += slim_in[e][c:c + 1, :]
                elif dx:
                    drag_sum[c, x0] += slim_in[e][c]
                else:
                    for x in range(cx):
                        drag_sum[c, x, y0:y0 + 1, :] += slim_in[e][c, x:x + 1, :]
            for copy in copies:
                copy.wait_send()

    gain = g_ext[...]
    offset = gain * (s_ext[...] + 2.0 * load[...])
    value = p_ext[...]
    wx, wy, depth = value.shape
    lane = lax.broadcasted_iota(jnp.int32, (wx * wy, depth), 1)
    first, last = lane == 0, lane == depth - 1
    edge_x = jnp.zeros((1, wy, depth), f32)
    for sweep in range(ITERS):
        flat = value.reshape(wx * wy, depth)
        near = (jnp.where(first, 0.0, pltpu.roll(flat, 1, 1))
                + jnp.where(last, 0.0, pltpu.roll(flat, depth - 1, 1)))
        near = near + pltpu.roll(flat, 1, 0) + pltpu.roll(flat, wx * wy - 1, 0)
        near = near.reshape(wx, wy, depth)
        near = near + jnp.concatenate([edge_x, value[:-1]], axis=0)
        near = near + jnp.concatenate([value[1:], edge_x], axis=0)
        value = gain * near + offset
    press[...] = value[WIDE:WIDE + cx, WIDE:WIDE + cy, :]


def shapes(cx, cy, depth, thick):
    wide = [VM(thick + (cx if dx == 0 else WIDE, cy if dy == 0 else WIDE, depth), f32)
            for dx, dy in AROUND]
    return wide + wide


def slim_shapes(cx, cy, depth):
    slim = [VM((8, depth), f32) if dx and dy else VM((3, cy if dx else cx, depth), f32)
            for dx, dy in AROUND]
    return slim + slim


def body(n_x, n_y, particles, send_list, move_count, tile_pairs, tile_count, drag_tiles,
         cell_slot, fluid_velocity, pressure_init, source, solid_old, screening):
    own = particles[0, 0]
    n_own, comps, width = own.shape
    slots = send_list.shape[3]
    pool = n_own + 4 * slots
    cx, cy, depth = pressure_init.shape
    n = len(AROUND)
    send = send_list.reshape(-1)
    sds = jax.ShapeDtypeStruct
    vmem = pl.BlockSpec(memory_space=VM)
    smem = pl.BlockSpec(memory_space=pltpu.SMEM)

    blocks = pl.pallas_call(
        pick_kernel, out_shape=sds((4 * slots, comps, width), f32),
        in_specs=[smem, vmem], out_specs=vmem,
    )(send, own).reshape(4, slots, comps, width)

    ext = (cx + 2 * WIDE, cy + 2 * WIDE, depth)
    column_rows = (cx + 2) * (cy + 2) * 8
    got, columns, p_ext, g_ext, s_ext = pl.pallas_call(
        functools.partial(exchange_kernel, n_x, n_y),
        out_shape=[sds((4, slots, comps, width), f32), sds((column_rows, depth), f32),
                   sds(ext, f32), sds(ext, f32), sds(ext, f32)],
        in_specs=[vmem] * 6, out_specs=[vmem] * 5,
        scratch_shapes=shapes(cx, cy, depth, (3,)) + slim_shapes(cx, cy, depth)
        + [pltpu.SemaphoreType.DMA((2 * n + 4,)), pltpu.SemaphoreType.DMA((2 * n + 4,))],
        compiler_params=pltpu.CompilerParams(collective_id=0, has_side_effects=True,
                                             vmem_limit_bytes=LIMIT),
    )(blocks, fluid_velocity, pressure_init, screening, source, solid_old)

    deposit, force = pl.pallas_call(
        forces_kernel,
        out_shape=[sds((4, cx + 2, cy + 2, depth), f32), sds((pool, 3, width), f32)],
        in_specs=[smem] * 5 + [vmem] * 4, out_specs=[vmem] * 2,
        scratch_shapes=[pltpu.SMEM((n_own,), f32), VM((pool, 32, width), bf16),
                        VM((pool, 32, 2 * width), bf16), VM((pool, 16, 2 * width), bf16),
                        VM((pool, 8, width), f32), VM((pool, 8, width), f32),
                        VM((column_rows, depth), f32)],
        compiler_params=pltpu.CompilerParams(vmem_limit_bytes=LIMIT),
    )(tile_pairs.reshape(-1), tile_count.reshape(-1), drag_tiles.reshape(-1), send,
      move_count.reshape(-1), own, got, cell_slot[0, 0], columns)

    press, drag_sum = pl.pallas_call(
        functools.partial(pressure_kernel, n_x, n_y),
        out_shape=[sds((cx, cy, depth), f32), sds((3, cx, cy, depth), f32)],
        in_specs=[vmem] * 4, out_specs=[vmem] * 2,
        scratch_shapes=[VM(ext, f32)] + shapes(cx + 2, cy + 2, depth, ())
        + slim_shapes(cx, cy, depth)
        + [pltpu.SemaphoreType.DMA((2 * n,)), pltpu.SemaphoreType.DMA((2 * n,))],
        compiler_params=pltpu.CompilerParams(collective_id=1, has_side_effects=True,
                                             vmem_limit_bytes=LIMIT),
    )(deposit, p_ext, g_ext, s_ext)
    return press, drag_sum, force[None, None]


def solution(mesh):
    tail = P("gx", "gy", None)
    in_specs = (
        P("gx", "gy", None, None, None),
        P("gx", "gy", None, None),
        P("gx", "gy", None, None),
        P("gx", "gy", None, None),
        P("gx", "gy"),
        P("gx", "gy", None, None),
        P("gx", "gy", None, None),
        P(None, "gx", "gy", None),
        tail, tail, tail, tail,
    )
    out_specs = (tail, P(None, "gx", "gy", None), P("gx", "gy", None, None, None))
    return jax.shard_map(functools.partial(body, mesh.shape["gx"], mesh.shape["gy"]), mesh=mesh,
                         in_specs=in_specs, out_specs=out_specs, check_vma=False)
```

time: 396 us -> 141 us (0.36)
  matrix products: 150 us -> 0 us
  Pallas kernels: 0 us -> 133 us
  other arithmetic: 101 us -> 0 us
  starting transfers between devices: 79.3 us -> 0 us
  local copies, waits for them, and re-layouts: 40.4 us -> 6.55 us
  waiting for transfers between devices: 19.1 us -> 0 us
    dot_general x34 -> x0, matrix products: 150 us -> none  [the longest x16 104 us: tile_step(): jnp.einsum('tab,tcb->tca', weight, second_side[:, 0:3, :], precision=topm...]
    pallas_call x0 -> x4, Pallas kernels: none -> 133 us  [the longest x1 74.5 us: body(): pl.pallas_call(functools.partial(pressure_kernel, n_x, n_y), out_shape=[s...]
    ppermute x28 -> x0, starting transfers between devices: 79.3 us -> none  [the longest x14 40.9 us: extended_2(): lax.ppermute(lax.slice_in_dim(block, 0, width, axis=dim), axis, backward)]
    reduce_sum x16 -> x0, other arithmetic: 52.2 us -> none  [tile_step(): pushed = first_side[:, 0:3, :] * jnp.sum(weight, axis=2)[:, None, :]]
    gather x39 -> x0, local copies, waits for them, and re-layouts: 29.2 us -> none  [the longest x16 10.7 us: tile_step(): second_side = block_pool[pair_group[:, 1], 0:4, :]]
    scatter-add x24 -> x0, other arithmetic: 28.5 us -> none  [the longest x16 26.4 us: tile_step(): force_total.at[pair_group[:, 0]].add(stiffness * (pushed - pulled))]
    ppermute x28 -> x0, waiting for transfers between devices: 19.1 us -> none  [the longest x14 11.4 us: extended_2(): lax.ppermute(lax.slice_in_dim(block, block.shape[dim] - width, None, axis...]
    select_n x19 -> x0, other arithmetic: 10.1 us -> none  [the longest x6 4.73 us: group_advance(): slot_tile = group_slots // depth_count]
  transfers between devices with their start and end apart: 28 -> 0, of which waited for: 10 -> 0; matrix products, arithmetic and copies ran while one was open for 72% -> 0% of each run, Pallas kernels for 0% -> 0%
where the time goes in v1:
time: 141 us
  Pallas kernels  133 us (94%)
  local copies, waits for them, and re-layouts  6.55 us (5%)
  between operations  1.46 us (1%)
    pallas_call x1, Pallas kernels, body(): pl.pallas_call(functools.partial(pressure_kernel, n_x, n_y), out_shape=[s...  74.5 us
    pallas_call x1, Pallas kernels, body(): pl.pallas_call(forces_kernel, out_shape=[sds((4, cx + 2, cy + 2, depth),...  41.6 us
    pallas_call x1, Pallas kernels, body(): pl.pallas_call(functools.partial(exchange_kernel, n_x, n_y), out_shape=[s...  14.2 us
    unnamed x31, local copies, waits for them, and re-layouts  5.51 us

profile of v1, /device:TPU:12, one launch (start us, length us, event | category | flops | bytes accessed | tf_op | source)
XLA Modules:
  0.0 140.8 jit_solution(17725014240275231215)
XLA Ops:
  0.6 0.0 copy-start.9
  1.3 0.0 copy-start.12
  1.3 0.0 copy-start.11
  1.3 0.7 copy-done.12
  2.0 0.1 reshape.28.moves
  2.1 0.0 copy-done.11
  2.1 0.6 reshape.27.send_ref.send
  2.7 0.0 copy-done.9
  2.7 0.1 copy.17
  2.9 0.0 copy-start.10
  2.9 0.1 reshape.26.tiles
  3.0 0.5 copy-done.10
  3.5 0.1 copy.16
  3.7 0.2 reshape.24.pairs
  3.9 0.0 copy-start.3
  3.9 0.0 copy-start.4
  3.9 0.0 copy-start.5
  3.9 0.0 copy-start.6
  3.9 0.0 copy-start.7
  3.9 2.5 %shard_map.139 = f32[256,8,128]{2,1,0:T(8,128)} custom-call(s32[256]{0:T(256)} %reshape.27.send_ref.send, f32[128,8,128]{2,1,0:T(8,128)} %bitcast.11), custom_call_target="tpu_custom_call" | custom-call | tf_op jit(solution)/shard_map/pallas_call | solution.py:472
  6.5 0.0 copy-done.3
  6.5 0.0 copy-done.4
  6.5 0.0 copy-done.5
  6.5 0.0 copy-done.6
  6.5 0.0 copy-done.7
  6.5 0.0 copy-start
  6.5 1.2 copy-done
  7.7 0.0 copy-start.1
  7.7 0.0 copy-start.2
  7.7 14.2 %shard_map.140 = (f32[4,64,8,128]{3,2,1,0:T(8,128)S(1)}, f32[800,128]{1,0:T(8,128)S(1)}, f32[16,16,128]{2,1,0:T(8,128)S(1)}, f32[16,16,128]{2,1,0:T(8,128)S(1)}, f32[16,16,128]{2,1,0:T(8,128)S(1)}) custom-call(f32[4,64,8,128]{3,2,1,0:T(8,128)S(1)} %bitcast.10, f32[3,8,8,128]{3,2,1,0:T(8,128)S(1)} %copy-done.3, f32[8,8,128]{2,1,0:T(8,128)S(1)} %copy-done.4, ...), custom_call_target="tpu_custom_call" | custom-call | tf_op jit(solution)/shard_map/pallas_call | solution.py:479
  21.9 0.0 copy-start.8
  21.9 0.0 copy-done.1
  21.9 0.0 copy-done.2
  21.9 0.7 copy-done.8
  22.6 41.6 %shard_map.141 = (f32[4,10,10,128]{3,2,1,0:T(8,128)S(1)}, f32[384,3,128]{2,1,0:T(4,128)S(1)}) custom-call(s32[1024]{0:T(1024)S(1)} %reshape.24.pairs, s32[1]{0:T(128)} %bitcast.9.count, s32[1536]{0:T(1024)S(1)} %reshape.26.tiles, s32[256]{0:T(256)S(1)} %copy-done.8, s32[8]{0:T(128)S(1)} %reshape.28.moves, f32[128,8,128]{2,1,0:T(8,128)S(1)} %bitcast.12, ...), custom_call_target="tpu_custom_call" | custom-call | tf_op jit(solution)/shard_map/pallas_call | solution.py:490
  64.2 74.5 %shard_map.142 = (f32[8,8,128]{2,1,0:T(8,128)S(1)}, f32[3,8,8,128]{3,2,1,0:T(8,128)S(1)}) custom-call(f32[4,10,10,128]{3,2,1,0:T(8,128)S(1)} %get-tuple-element.14.deposit, f32[16,16,128]{2,1,0:T(8,128)S(1)} %get-tuple-element.15.p_ext, f32[16,16,128]{2,1,0:T(8,128)S(1)} %get-tuple-element.16.g_ext, f32[16,16,128]{2,1,0:T(8,128)S(1)} %get-tuple-element.17.s_ext), custom_call_target="tpu_custom_call" | custom-call | tf_op jit(solution)/shard_map/pallas_call | solution.py:502
  138.7 0.9 copy.18
  139.6 0.6 copy.22
  140.2 0.6 copy.23
Async XLA Ops:
  0.6 2.1 %copy-start.9 = (s32[1,1,384,4]{2,3,1,0:T(4,128)S(1)}, s32[1,1,384,4]{2,3,1,0:T(4,128)}, u32[]{:S(2)}) copy-start(s32[1,1,384,4]{2,3,1,0:T(4,128)} %param.17) | copy-start | bytes 18436
  1.3 0.7 copy-start.12
  1.3 0.8 copy-start.11
  2.9 0.7 copy-start.10
  3.9 2.6 %copy-start.3 = (f32[3,8,8,128]{3,2,1,0:T(8,128)S(1)}, f32[3,8,8,128]{3,2,1,0:T(8,128)}, u32[]{:S(2)}) copy-start(f32[3,8,8,128]{3,2,1,0:T(8,128)} %flow.1) | copy-start | bytes 294916
  3.9 2.6 %copy-start.4 = (f32[8,8,128]{2,1,0:T(8,128)S(1)}, f32[8,8,128]{2,1,0:T(8,128)}, u32[]{:S(2)}) copy-start(f32[8,8,128]{2,1,0:T(8,128)} %press.1) | copy-start | bytes 98308
  3.9 2.6 %copy-start.5 = (f32[8,8,128]{2,1,0:T(8,128)S(1)}, f32[8,8,128]{2,1,0:T(8,128)}, u32[]{:S(2)}) copy-start(f32[8,8,128]{2,1,0:T(8,128)} %screen.1) | copy-start | bytes 98308
  3.9 2.6 %copy-start.6 = (f32[8,8,128]{2,1,0:T(8,128)S(1)}, f32[8,8,128]{2,1,0:T(8,128)}, u32[]{:S(2)}) copy-start(f32[8,8,128]{2,1,0:T(8,128)} %source.1) | copy-start | bytes 98308
  3.9 2.6 %copy-start.7 = (f32[8,8,128]{2,1,0:T(8,128)S(1)}, f32[8,8,128]{2,1,0:T(8,128)}, u32[]{:S(2)}) copy-start(f32[8,8,128]{2,1,0:T(8,128)} %solid.1) | copy-start | bytes 98308
  6.5 1.2 copy-start
  7.7 14.2 %copy-start.1 = (f32[1,1,128,8,128]{4,3,2,1,0:T(8,128)S(1)}, f32[1,1,128,8,128]{4,3,2,1,0:T(8,128)}, u32[]{:S(2)}) copy-start(f32[1,1,128,8,128]{4,3,2,1,0:T(8,128)} %param.12) | copy-start | bytes 1572868
  7.7 14.2 %copy-start.2 = (s32[1,1,384,128]{3,2,1,0:T(8,128)S(1)}, s32[1,1,384,128]{3,2,1,0:T(8,128)}, u32[]{:S(2)}) copy-start(s32[1,1,384,128]{3,2,1,0:T(8,128)} %param.18) | copy-start | bytes 589828
  21.9 0.7 copy-start.8

commit v2 on v1

--- a/solution.py
+++ b/solution.py
@@ -184,15 +184,8 @@
             copy.wait_send()
 
 
-def split3(value):
-    high = value.astype(bf16).astype(f32)
-    rest = value - high
-    mid = rest.astype(bf16).astype(f32)
-    return high, mid, (rest - mid).astype(bf16).astype(f32)
-
-
 def forces_kernel(pairs, count, tiles, send, moves, own, got, cells, columns,
-                  deposit, force, owned, tab_a, tab_b, tab_y, total, drag, dep):
+                  deposit, force, owned, whole, column, tab_y, total, drag, dep):
     n_own, slots = own.shape[0], got.shape[1]
     pool = n_own + 4 * slots
     cx, cy = deposit.shape[1], deposit.shape[2]
@@ -216,28 +209,14 @@
     total[...] = jnp.zeros(total.shape, f32)
 
     def tables(m, block):
-        both = jnp.where(low, block, pltpu.roll(block, 4, 0))
-        c1, c2, c3 = split3(both)
-        square = jnp.where(row < 3, -both * both, jnp.where(row == 3, both * both, 0.0))
-        n1, n2, n3 = split3(jnp.sum(square, axis=0, keepdims=True))
-        ones = jnp.ones((8, depth), f32)
-        zeros = jnp.zeros((8, depth), f32)
-        a3 = jnp.where(row == 0, n1, jnp.where(row == 1, n2, jnp.where(row == 2, n3, jnp.where(row < 6, ones, zeros))))
-        b3 = jnp.where(row == 3, n1, jnp.where(row == 4, n2, jnp.where(row == 5, n3, jnp.where(row < 3, ones, zeros))))
-        a = jnp.concatenate([c1, c2, jnp.where(low, c1, c3), a3], axis=0)
-        twice = 2.0 * jnp.where(low, c1, c2)
-        b = jnp.concatenate([twice, twice, 2.0 * jnp.where(low, c3, c1), b3], axis=0)
-        third = jnp.where(row == 3, ones, zeros)
-        r1, r2, r3 = c1[3:4], c2[3:4], c3[3:4]
-        reach = jnp.where(row == 3, r1, jnp.where(row == 4, r2, jnp.where(row == 5, r3, zeros)))
-        r = jnp.concatenate([third, third, jnp.where(row == 7, ones, zeros), reach], axis=0)
-        y1 = jnp.where(row < 3, c1, jnp.where(row == 3, ones, jnp.where(row < 7, c2, zeros)))
-        y2 = jnp.where(row < 3, c1, jnp.where(row == 3, ones, zeros))
-        y = jnp.concatenate([jnp.concatenate([y1, y2], axis=1),
-                             jnp.zeros((8, 2 * depth), f32)], axis=0)
-        tab_a[m] = a.astype(bf16)
-        tab_b[m] = jnp.concatenate([b, r], axis=1).astype(bf16)
-        tab_y[m] = y.astype(bf16)
+        whole[m] = block
+        column[m] = block.T
+        ones = jnp.where(row < 3, block, jnp.where(row == 3, 1.0, 0.0))
+        high = ones.astype(bf16).astype(f32)
+        rest = pltpu.roll(ones - high, 4, 0)
+        high = jnp.where(row < 4, high, 0.0)
+        y = jnp.concatenate([jnp.where(low, high, rest), high], axis=1)
+        tab_y[m] = jnp.concatenate([y, jnp.zeros((8, 2 * depth), f32)], axis=0).astype(bf16)
 
     def drag_block(m, block, cell, mine):
         slot = cell // depth
@@ -309,12 +288,13 @@
         for u in range(UNROLL):
             t = s * UNROLL + u
             i, j = pairs[2 * t], pairs[2 * t + 1]
-            mr = lax.dot_general(tab_a[j], tab_b[i], (((0,), (0,)), ((), ())),
-                                 preferred_element_type=f32)
-            over, reach = mr[:, :depth], mr[:, depth:]
+            first, second = whole[i], column[j]
+            gap = [second[:, c:c + 1] - first[c:c + 1, :] for c in range(3)]
+            apart = gap[0] * gap[0] + gap[1] * gap[1] + gap[2] * gap[2]
+            reach = second[:, 3:4] + first[3:4, :]
+            reach = reach * reach
             inverse = pl.reciprocal(reach, approx=True)
-            inverse = inverse * (2.0 - reach * inverse)
-            weight = jnp.maximum(over, 0.0) * (inverse * inverse)
+            weight = jnp.maximum(1.0 - apart * inverse, 0.0)
             w1 = weight.astype(bf16)
             w2 = (weight - w1.astype(f32)).astype(bf16)
             out = lax.dot_general(tab_y[j], jnp.concatenate([w1, w2], axis=0),
@@ -491,8 +471,8 @@
         forces_kernel,
         out_shape=[sds((4, cx + 2, cy + 2, depth), f32), sds((pool, 3, width), f32)],
         in_specs=[smem] * 5 + [vmem] * 4, out_specs=[vmem] * 2,
-        scratch_shapes=[pltpu.SMEM((n_own,), f32), VM((pool, 32, width), bf16),
-                        VM((pool, 32, 2 * width), bf16), VM((pool, 16, 2 * width), bf16),
+        scratch_shapes=[pltpu.SMEM((n_own,), f32), VM((pool, comps, width), f32),
+                        VM((pool, width, comps), f32), VM((pool, 16, 2 * width), bf16),
                         VM((pool, 8, width), f32), VM((pool, 8, width), f32),
                         VM((column_rows, depth), f32)],
         compiler_params=pltpu.CompilerParams(vmem_limit_bytes=LIMIT),

time: 141 us -> 102 us (0.72)
  Pallas kernels: 133 us -> 93.8 us
    pallas_call x1, Pallas kernels: 74.5 us -> 38 us  [body(): pl.pallas_call(functools.partial(pressure_kernel, n_x, n_y), out_shape=[s...]
    pallas_call x1, Pallas kernels: 41.6 us -> 39 us  [body(): pl.pallas_call(forces_kernel, out_shape=[sds((4, cx + 2, cy + 2, depth),...]
where the time goes in v2:
time: 102 us
  Pallas kernels  93.8 us (92%)
  local copies, waits for them, and re-layouts  6.55 us (6%)
  between operations  1.46 us (1%)
    pallas_call x1, Pallas kernels, body(): pl.pallas_call(forces_kernel, out_shape=[sds((4, cx + 2, cy + 2, depth),...  39 us
    pallas_call x1, Pallas kernels, body(): pl.pallas_call(functools.partial(pressure_kernel, n_x, n_y), out_shape=[s...  38 us
    pallas_call x1, Pallas kernels, body(): pl.pallas_call(functools.partial(exchange_kernel, n_x, n_y), out_shape=[s...  14.2 us
    unnamed x31, local copies, waits for them, and re-layouts  5.51 us
    pallas_call x1, Pallas kernels, body(): pl.pallas_call(pick_kernel, out_shape=sds((4 * slots, comps, width), f32)...  2.54 us

profile of v2, /device:TPU:12, one launch (start us, length us, event | category | flops | bytes accessed | tf_op | source)
XLA Modules:
  0.0 101.8 jit_solution(11750368405571325093)
XLA Ops:
  0.6 0.0 copy-start.9
  1.3 0.0 copy-start.12
  1.3 0.0 copy-start.11
  1.3 0.7 copy-done.12
  2.0 0.1 reshape.28.moves
  2.1 0.0 copy-done.11
  2.1 0.6 reshape.27.send_ref.send
  2.7 0.0 copy-done.9
  2.7 0.1 copy.17
  2.9 0.0 copy-start.10
  2.9 0.1 reshape.26.tiles
  3.0 0.5 copy-done.10
  3.5 0.1 copy.16
  3.7 0.2 reshape.24.pairs
  3.9 0.0 copy-start.3
  3.9 0.0 copy-start.4
  3.9 0.0 copy-start.5
  3.9 0.0 copy-start.6
  3.9 0.0 copy-start.7
  3.9 2.5 %shard_map.139 = f32[256,8,128]{2,1,0:T(8,128)} custom-call(s32[256]{0:T(256)} %reshape.27.send_ref.send, f32[128,8,128]{2,1,0:T(8,128)} %bitcast.11), custom_call_target="tpu_custom_call" | custom-call | tf_op jit(solution)/shard_map/pallas_call | solution.py:452
  6.5 0.0 copy-done.3
  6.5 0.0 copy-done.4
  6.5 0.0 copy-done.5
  6.5 0.0 copy-done.6
  6.5 0.0 copy-done.7
  6.5 0.0 copy-start
  6.5 1.2 %copy-done = f32[256,8,128]{2,1,0:T(8,128)S(1)} copy-done((f32[256,8,128]{2,1,0:T(8,128)S(1)}, f32[256,8,128]{2,1,0:T(8,128)}, u32[]{:S(2)}) %copy-start) | copy-done | bytes 1048600
  7.7 0.0 copy-start.1
  7.7 0.0 copy-start.2
  7.7 14.2 %shard_map.140 = (f32[4,64,8,128]{3,2,1,0:T(8,128)S(1)}, f32[800,128]{1,0:T(8,128)S(1)}, f32[16,16,128]{2,1,0:T(8,128)S(1)}, f32[16,16,128]{2,1,0:T(8,128)S(1)}, f32[16,16,128]{2,1,0:T(8,128)S(1)}) custom-call(f32[4,64,8,128]{3,2,1,0:T(8,128)S(1)} %bitcast.10, f32[3,8,8,128]{3,2,1,0:T(8,128)S(1)} %copy-done.3, f32[8,8,128]{2,1,0:T(8,128)S(1)} %copy-done.4, ...), custom_call_target="tpu_custom_call" | custom-call | tf_op jit(solution)/shard_map/pallas_call | solution.py:459
  21.9 0.0 copy-start.8
  21.9 0.0 copy-done.1
  21.9 0.0 copy-done.2
  21.9 0.7 copy-done.8
  22.6 39.0 %shard_map.141 = (f32[4,10,10,128]{3,2,1,0:T(8,128)S(1)}, f32[384,3,128]{2,1,0:T(4,128)S(1)}) custom-call(s32[1024]{0:T(1024)S(1)} %reshape.24.pairs, s32[1]{0:T(128)} %bitcast.9.count, s32[1536]{0:T(1024)S(1)} %reshape.26.tiles, s32[256]{0:T(256)S(1)} %copy-done.8, s32[8]{0:T(128)S(1)} %reshape.28.moves, f32[128,8,128]{2,1,0:T(8,128)S(1)} %bitcast.12, ...), custom_call_target="tpu_custom_call" | custom-call | tf_op jit(solution)/shard_map/pallas_call | solution.py:470
  61.7 38.0 %shard_map.142 = (f32[8,8,128]{2,1,0:T(8,128)S(1)}, f32[3,8,8,128]{3,2,1,0:T(8,128)S(1)}) custom-call(f32[4,10,10,128]{3,2,1,0:T(8,128)S(1)} %get-tuple-element.14.deposit, f32[16,16,128]{2,1,0:T(8,128)S(1)} %get-tuple-element.15.p_ext, f32[16,16,128]{2,1,0:T(8,128)S(1)} %get-tuple-element.16.g_ext, f32[16,16,128]{2,1,0:T(8,128)S(1)} %get-tuple-element.17.s_ext), custom_call_target="tpu_custom_call" | custom-call | tf_op jit(solution)/shard_map/pallas_call | solution.py:482
  99.7 0.9 copy.18
  100.5 0.6 copy.22
  101.1 0.6 copy.23
Async XLA Ops:
  0.6 2.1 %copy-start.9 = (s32[1,1,384,4]{2,3,1,0:T(4,128)S(1)}, s32[1,1,384,4]{2,3,1,0:T(4,128)}, u32[]{:S(2)}) copy-start(s32[1,1,384,4]{2,3,1,0:T(4,128)} %param.17) | copy-start | bytes 18436
  1.3 0.7 copy-start.12
  1.3 0.8 copy-start.11
  2.9 0.7 copy-start.10
  3.9 2.6 %copy-start.3 = (f32[3,8,8,128]{3,2,1,0:T(8,128)S(1)}, f32[3,8,8,128]{3,2,1,0:T(8,128)}, u32[]{:S(2)}) copy-start(f32[3,8,8,128]{3,2,1,0:T(8,128)} %flow.1) | copy-start | bytes 294916
  3.9 2.6 %copy-start.4 = (f32[8,8,128]{2,1,0:T(8,128)S(1)}, f32[8,8,128]{2,1,0:T(8,128)}, u32[]{:S(2)}) copy-start(f32[8,8,128]{2,1,0:T(8,128)} %press.1) | copy-start | bytes 98308
  3.9 2.6 %copy-start.5 = (f32[8,8,128]{2,1,0:T(8,128)S(1)}, f32[8,8,128]{2,1,0:T(8,128)}, u32[]{:S(2)}) copy-start(f32[8,8,128]{2,1,0:T(8,128)} %screen.1) | copy-start | bytes 98308
  3.9 2.6 %copy-start.6 = (f32[8,8,128]{2,1,0:T(8,128)S(1)}, f32[8,8,128]{2,1,0:T(8,128)}, u32[]{:S(2)}) copy-start(f32[8,8,128]{2,1,0:T(8,128)} %source.1) | copy-start | bytes 98308
  3.9 2.6 %copy-start.7 = (f32[8,8,128]{2,1,0:T(8,128)S(1)}, f32[8,8,128]{2,1,0:T(8,128)}, u32[]{:S(2)}) copy-start(f32[8,8,128]{2,1,0:T(8,128)} %solid.1) | copy-start | bytes 98308
  6.5 1.2 %copy-start = (f32[256,8,128]{2,1,0:T(8,128)S(1)}, f32[256,8,128]{2,1,0:T(8,128)}, u32[]{:S(2)}) copy-start(f32[256,8,128]{2,1,0:T(8,128)} %shard_map.139) | copy-start | bytes 3145732
  7.7 14.2 %copy-start.1 = (f32[1,1,128,8,128]{4,3,2,1,0:T(8,128)S(1)}, f32[1,1,128,8,128]{4,3,2,1,0:T(8,128)}, u32[]{:S(2)}) copy-start(f32[1,1,128,8,128]{4,3,2,1,0:T(8,128)} %param.12) | copy-start | bytes 1572868
  7.7 14.2 %copy-start.2 = (s32[1,1,384,128]{3,2,1,0:T(8,128)S(1)}, s32[1,1,384,128]{3,2,1,0:T(8,128)}, u32[]{:S(2)}) copy-start(s32[1,1,384,128]{3,2,1,0:T(8,128)} %param.18) | copy-start | bytes 589828
  21.9 0.7 copy-start.8

commit v3 on v2

--- a/solution.py
+++ b/solution.py
@@ -10,7 +10,8 @@
 ITERS = 4
 MOVERS = 16
 WIDE = ITERS
-UNROLL = 8
+UNROLL = 16
+CHUNK = 16
 MESH = pl.DeviceIdType.MESH
 AROUND = [(dx, dy) for dx in (-1, 0, 1) for dy in (-1, 0, 1) if (dx, dy) != (0, 0)]
 GROUPS = [(1, 0), (-1, 0), (0, 1), (0, -1)]
@@ -289,15 +290,18 @@
             t = s * UNROLL + u
             i, j = pairs[2 * t], pairs[2 * t + 1]
             first, second = whole[i], column[j]
-            gap = [second[:, c:c + 1] - first[c:c + 1, :] for c in range(3)]
-            apart = gap[0] * gap[0] + gap[1] * gap[1] + gap[2] * gap[2]
-            reach = second[:, 3:4] + first[3:4, :]
-            reach = reach * reach
-            inverse = pl.reciprocal(reach, approx=True)
-            weight = jnp.maximum(1.0 - apart * inverse, 0.0)
-            w1 = weight.astype(bf16)
-            w2 = (weight - w1.astype(f32)).astype(bf16)
-            out = lax.dot_general(tab_y[j], jnp.concatenate([w1, w2], axis=0),
+            highs, rests = [], []
+            for h in range(0, depth, CHUNK):
+                part = second[h:h + CHUNK]
+                gap = [part[:, c:c + 1] - first[c:c + 1, :] for c in range(3)]
+                apart = gap[0] * gap[0] + gap[1] * gap[1] + gap[2] * gap[2]
+                reach = part[:, 3:4] + first[3:4, :]
+                inverse = pl.reciprocal(reach * reach, approx=True)
+                weight = jnp.maximum(1.0 - apart * inverse, 0.0)
+                high = weight.astype(bf16)
+                highs.append(high)
+                rests.append((weight - high.astype(f32)).astype(bf16))
+            out = lax.dot_general(tab_y[j], jnp.concatenate(highs + rests, axis=0),
                                   (((1,), (0,)), ((), ())), preferred_element_type=f32)
             keep = jnp.where(t < count[0], 1.0, 0.0).astype(f32)
             results.append((i, out[0:8] * keep))

time: 102 us -> 109 us (1.069)
  Pallas kernels: 93.8 us -> 101 us
    pallas_call x1, Pallas kernels: 38 us -> 48.2 us  [body(): pl.pallas_call(functools.partial(pressure_kernel, n_x, n_y), out_shape=[s...]
    pallas_call x1, Pallas kernels: 39 us -> 36.3 us  [body(): pl.pallas_call(forces_kernel, out_shape=[sds((4, cx + 2, cy + 2, depth),...]
where the time goes in v3:
time: 109 us
  Pallas kernels  101 us (93%)
  local copies, waits for them, and re-layouts  6.55 us (6%)
  between operations  1.46 us (1%)
    pallas_call x1, Pallas kernels, body(): pl.pallas_call(functools.partial(pressure_kernel, n_x, n_y), out_shape=[s...  48.2 us
    pallas_call x1, Pallas kernels, body(): pl.pallas_call(forces_kernel, out_shape=[sds((4, cx + 2, cy + 2, depth),...  36.3 us
    pallas_call x1, Pallas kernels, body(): pl.pallas_call(functools.partial(exchange_kernel, n_x, n_y), out_shape=[s...  14.2 us
    unnamed x31, local copies, waits for them, and re-layouts  5.51 us
    pallas_call x1, Pallas kernels, body(): pl.pallas_call(pick_kernel, out_shape=sds((4 * slots, comps, width), f32)...  2.54 us

profile of v3, /device:TPU:12, one launch (start us, length us, event | category | flops | bytes accessed | tf_op | source)
XLA Modules:
  0.0 109.2 jit_solution(13394277195425345236)
XLA Ops:
  0.6 0.0 copy-start.9
  1.3 0.0 copy-start.12
  1.3 0.0 copy-start.11
  1.3 0.7 copy-done.12
  2.0 0.1 reshape.28.moves
  2.1 0.0 copy-done.11
  2.1 0.6 reshape.27.send_ref.send
  2.7 0.0 copy-done.9
  2.7 0.1 copy.17
  2.9 0.0 copy-start.10
  2.9 0.1 reshape.26.tiles
  3.0 0.5 copy-done.10
  3.5 0.1 copy.16
  3.7 0.2 reshape.24.pairs
  3.9 0.0 copy-start.3
  3.9 0.0 copy-start.4
  3.9 0.0 copy-start.5
  3.9 0.0 copy-start.6
  3.9 0.0 copy-start.7
  3.9 2.5 %shard_map.139 = f32[256,8,128]{2,1,0:T(8,128)} custom-call(s32[256]{0:T(256)} %reshape.27.send_ref.send, f32[128,8,128]{2,1,0:T(8,128)} %bitcast.11), custom_call_target="tpu_custom_call" | custom-call | tf_op jit(solution)/shard_map/pallas_call | solution.py:456
  6.5 0.0 copy-done.3
  6.5 0.0 copy-done.4
  6.5 0.0 copy-done.5
  6.5 0.0 copy-done.6
  6.5 0.0 copy-done.7
  6.5 0.0 copy-start
  6.5 1.2 %copy-done = f32[256,8,128]{2,1,0:T(8,128)S(1)} copy-done((f32[256,8,128]{2,1,0:T(8,128)S(1)}, f32[256,8,128]{2,1,0:T(8,128)}, u32[]{:S(2)}) %copy-start) | copy-done | bytes 1048600
  7.7 0.0 copy-start.1
  7.7 0.0 copy-start.2
  7.7 14.2 %shard_map.140 = (f32[4,64,8,128]{3,2,1,0:T(8,128)S(1)}, f32[800,128]{1,0:T(8,128)S(1)}, f32[16,16,128]{2,1,0:T(8,128)S(1)}, f32[16,16,128]{2,1,0:T(8,128)S(1)}, f32[16,16,128]{2,1,0:T(8,128)S(1)}) custom-call(f32[4,64,8,128]{3,2,1,0:T(8,128)S(1)} %bitcast.10, f32[3,8,8,128]{3,2,1,0:T(8,128)S(1)} %copy-done.3, f32[8,8,128]{2,1,0:T(8,128)S(1)} %copy-done.4, ...), custom_call_target="tpu_custom_call" | custom-call | tf_op jit(solution)/shard_map/pallas_call | solution.py:463
  21.9 0.0 copy-start.8
  21.9 0.0 copy-done.1
  21.9 0.0 copy-done.2
  21.9 0.7 copy-done.8
  22.6 36.3 %shard_map.141 = (f32[4,10,10,128]{3,2,1,0:T(8,128)S(1)}, f32[384,3,128]{2,1,0:T(4,128)S(1)}) custom-call(s32[1024]{0:T(1024)S(1)} %reshape.24.pairs, s32[1]{0:T(128)} %bitcast.9.count, s32[1536]{0:T(1024)S(1)} %reshape.26.tiles, s32[256]{0:T(256)S(1)} %copy-done.8, s32[8]{0:T(128)S(1)} %reshape.28.moves, f32[128,8,128]{2,1,0:T(8,128)S(1)} %bitcast.12, ...), custom_call_target="tpu_custom_call" | custom-call | tf_op jit(solution)/shard_map/pallas_call | solution.py:474
  58.9 48.2 %shard_map.142 = (f32[8,8,128]{2,1,0:T(8,128)S(1)}, f32[3,8,8,128]{3,2,1,0:T(8,128)S(1)}) custom-call(f32[4,10,10,128]{3,2,1,0:T(8,128)S(1)} %get-tuple-element.14.deposit, f32[16,16,128]{2,1,0:T(8,128)S(1)} %get-tuple-element.15.p_ext, f32[16,16,128]{2,1,0:T(8,128)S(1)} %get-tuple-element.16.g_ext, f32[16,16,128]{2,1,0:T(8,128)S(1)} %get-tuple-element.17.s_ext), custom_call_target="tpu_custom_call" | custom-call | tf_op jit(solution)/shard_map/pallas_call | solution.py:486
  107.1 0.9 copy.18
  107.9 0.6 copy.22
  108.5 0.6 copy.23
Async XLA Ops:
  0.6 2.1 %copy-start.9 = (s32[1,1,384,4]{2,3,1,0:T(4,128)S(1)}, s32[1,1,384,4]{2,3,1,0:T(4,128)}, u32[]{:S(2)}) copy-start(s32[1,1,384,4]{2,3,1,0:T(4,128)} %param.17) | copy-start | bytes 18436
  1.3 0.7 copy-start.12
  1.3 0.8 copy-start.11
  2.9 0.7 copy-start.10
  3.9 2.6 %copy-start.3 = (f32[3,8,8,128]{3,2,1,0:T(8,128)S(1)}, f32[3,8,8,128]{3,2,1,0:T(8,128)}, u32[]{:S(2)}) copy-start(f32[3,8,8,128]{3,2,1,0:T(8,128)} %flow.1) | copy-start | bytes 294916
  3.9 2.6 %copy-start.4 = (f32[8,8,128]{2,1,0:T(8,128)S(1)}, f32[8,8,128]{2,1,0:T(8,128)}, u32[]{:S(2)}) copy-start(f32[8,8,128]{2,1,0:T(8,128)} %press.1) | copy-start | bytes 98308
  3.9 2.6 %copy-start.5 = (f32[8,8,128]{2,1,0:T(8,128)S(1)}, f32[8,8,128]{2,1,0:T(8,128)}, u32[]{:S(2)}) copy-start(f32[8,8,128]{2,1,0:T(8,128)} %screen.1) | copy-start | bytes 98308
  3.9 2.6 %copy-start.6 = (f32[8,8,128]{2,1,0:T(8,128)S(1)}, f32[8,8,128]{2,1,0:T(8,128)}, u32[]{:S(2)}) copy-start(f32[8,8,128]{2,1,0:T(8,128)} %source.1) | copy-start | bytes 98308
  3.9 2.6 %copy-start.7 = (f32[8,8,128]{2,1,0:T(8,128)S(1)}, f32[8,8,128]{2,1,0:T(8,128)}, u32[]{:S(2)}) copy-start(f32[8,8,128]{2,1,0:T(8,128)} %solid.1) | copy-start | bytes 98308
  6.5 1.2 %copy-start = (f32[256,8,128]{2,1,0:T(8,128)S(1)}, f32[256,8,128]{2,1,0:T(8,128)}, u32[]{:S(2)}) copy-start(f32[256,8,128]{2,1,0:T(8,128)} %shard_map.139) | copy-start | bytes 3145732
  7.7 14.2 %copy-start.1 = (f32[1,1,128,8,128]{4,3,2,1,0:T(8,128)S(1)}, f32[1,1,128,8,128]{4,3,2,1,0:T(8,128)}, u32[]{:S(2)}) copy-start(f32[1,1,128,8,128]{4,3,2,1,0:T(8,128)} %param.12) | copy-start | bytes 1572868
  7.7 14.2 %copy-start.2 = (s32[1,1,384,128]{3,2,1,0:T(8,128)S(1)}, s32[1,1,384,128]{3,2,1,0:T(8,128)}, u32[]{:S(2)}) copy-start(s32[1,1,384,128]{3,2,1,0:T(8,128)} %param.18) | copy-start | bytes 589828
  21.9 0.7 copy-start.8
